TPU v7x, 256 devices: a whole 4x4x8 slice. The times are simulated.
256 devices in a mesh: blk: 64 (over y, x, z_hi), ma: 4 (over z_lo, core).
Axes of the slice: x: 4, y: 4, z: 8 (z_hi: 4, z_lo: 2; z = z_hi * 2 + z_lo), core: 2. Of those that a mesh axis runs over, the one named last changes fastest.
Arguments:
- white_noise: float32 [2560, 2, 2560], P(('ma', 'blk')), may hold values from -6 to 6
- amplitude: float32 [2560], replicated, may hold values from 0.002 to 0.015
- legendre: bfloat16 [128, 2560, 2560], P('blk', 'ma'), may hold values from -0.125 to 0.125
- order_of_slot: int32 [2560], replicated, may hold values from 0 to 2559, as said below
- counts: int32 [256, 8192], P(('blk', 'ma')), may hold values from 0 to 7
- survey_mask: int32 [256, 8192], P(('blk', 'ma')), may hold values from 0 to 1, as said below
Outputs:
- gradient: float32 [2560, 2, 2560], P(('ma', 'blk'))
Inputs may be any that keep to these rules, and one draw needn't show every extreme that they name: `order_of_slot`: a permutation of 0 to 2559 in which slots 2k and 2k+1 hold the orders m and 2559-m. `survey_mask`: every cycle row has at least one pixel equal to 1.
All inputs are finite; a program needn't handle non-finite values.
Results may differ from a plain program's by a relative error of at most 0.004.
Values may be sent and summed in bfloat16 or wider, within the bound.
A program may use at most 128 MiB of HBM per device.

v0:
```python
import jax
import jax.numpy as jnp
from jax import lax
from jax.sharding import PartitionSpec as P

exact_mode = lax.Precision.HIGHEST


def parity_signs(orders, degrees):
    degree = jnp.arange(degrees, dtype=jnp.int32)
    return jnp.where((degree[None, :] + orders[:, None]) % 2 == 0, 1.0, -1.0).astype(jnp.float32)


def circle(first_index, second_index, period):
    phase_turn = first_index[:, None] * second_index[None, :] % period
    phase_angle = 2.0 * jnp.pi / period * phase_turn.astype(jnp.float32)
    return (jnp.cos(phase_angle), jnp.sin(phase_angle))


def cycle_tables(total_slots, cycle_pixels):
    inner_len = cycle_pixels // 128
    outer_len = total_slots // 128
    fine_index = jnp.arange(128, dtype=jnp.int32)
    inner_index = jnp.arange(inner_len, dtype=jnp.int32)
    coarse_cos, coarse_sin = circle(jnp.arange(outer_len, dtype=jnp.int32), inner_index, inner_len)
    fine_cos, fine_sin = circle(fine_index, fine_index, 128)
    twiddle_cos, twiddle_sin = circle(inner_index, fine_index, cycle_pixels)
    return (coarse_cos, coarse_sin, fine_cos, fine_sin, twiddle_cos, twiddle_sin)


def to_field(spec_re, spec_im, tables):
    coarse_cos, coarse_sin, fine_cos, fine_sin, twiddle_cos, twiddle_sin = tables
    cycle_rows = spec_re.shape[0]
    outer_len = coarse_cos.shape[0]
    inner_len = coarse_cos.shape[1]
    parts_re = spec_re.reshape(cycle_rows, outer_len, 128)
    parts_im = spec_im.reshape(cycle_rows, outer_len, 128)
    section_re = jnp.einsum("rpq,pb->rbq", parts_re, coarse_cos, precision=exact_mode) - jnp.einsum(
        "rpq,pb->rbq", parts_im, coarse_sin, precision=exact_mode
    )
    section_im = jnp.einsum("rpq,pb->rbq", parts_re, coarse_sin, precision=exact_mode) + jnp.einsum(
        "rpq,pb->rbq", parts_im, coarse_cos, precision=exact_mode
    )
    twist_re = section_re * twiddle_cos - section_im * twiddle_sin
    twist_im = section_re * twiddle_sin + section_im * twiddle_cos
    plane_rows = jnp.einsum("rbq,qa->rba", twist_re, fine_cos, precision=exact_mode) - jnp.einsum(
        "rbq,qa->rba", twist_im, fine_sin, precision=exact_mode
    )
    return plane_rows.transpose(0, 2, 1).reshape(cycle_rows, 128 * inner_len)


def from_field(residual, tables):
    coarse_cos, coarse_sin, fine_cos, fine_sin, twiddle_cos, twiddle_sin = tables
    cycle_rows = residual.shape[0]
    outer_len = coarse_cos.shape[0]
    inner_len = coarse_cos.shape[1]
    cycle_grid = residual.reshape(cycle_rows, 128, inner_len)
    first_re = jnp.einsum("rab,qa->rbq", cycle_grid, fine_cos, precision=exact_mode)
    first_im = -jnp.einsum("rab,qa->rbq", cycle_grid, fine_sin, precision=exact_mode)
    turned_re = first_re * twiddle_cos + first_im * twiddle_sin
    turned_im = first_im * twiddle_cos - first_re * twiddle_sin
    modes_re = jnp.einsum("rbq,pb->rpq", turned_re, coarse_cos, precision=exact_mode) + jnp.einsum(
        "rbq,pb->rpq", turned_im, coarse_sin, precision=exact_mode
    )
    modes_im = jnp.einsum("rbq,pb->rpq", turned_im, coarse_cos, precision=exact_mode) - jnp.einsum(
        "rbq,pb->rpq", turned_re, coarse_sin, precision=exact_mode
    )
    return (
        modes_re.reshape(cycle_rows, outer_len * 128),
        modes_im.reshape(cycle_rows, outer_len * 128),
    )


def per_device(white_noise, amplitude, legendre, order_of_slot, counts, survey_mask):
    band_count = lax.axis_size("blk")
    cycle_band = lax.axis_index("blk")
    order_group = lax.axis_index("ma")
    north_rows = legendre.shape[0]
    block_slots = legendre.shape[1]
    degrees = legendre.shape[2]
    own_slots = white_noise.shape[0]
    total_slots = order_of_slot.shape[0]
    cycle_rows = counts.shape[0]
    cycle_pixels = counts.shape[1]
    block_orders = lax.dynamic_slice_in_dim(order_of_slot, order_group * block_slots, block_slots)
    own_orders = lax.dynamic_slice_in_dim(
        order_of_slot, (order_group * band_count + cycle_band) * own_slots, own_slots
    )
    degree = jnp.arange(degrees, dtype=jnp.int32)
    own_keep = degree[None, :] >= own_orders[:, None]
    harmonics = jnp.where(own_keep[:, None, :], amplitude[None, None, :] * white_noise, 0.0).astype(
        jnp.bfloat16
    )
    shard_rows = lax.all_gather(harmonics, "blk", axis=0, tiled=True)
    table_block = legendre
    piece_sign = parity_signs(block_orders, degrees)
    stacked = jnp.concatenate(
        [shard_rows, shard_rows * piece_sign.astype(jnp.bfloat16)[:, None, :]], axis=1
    )
    fourier = jnp.einsum("nsl,skl->kns", table_block, stacked, preferred_element_type=jnp.float32)
    fourier = (
        fourier.reshape(2, 2, north_rows, block_slots)
        .transpose(1, 0, 2, 3)
        .reshape(2, 2 * north_rows, block_slots)
    )
    rows_fourier = lax.all_to_all(fourier, "ma", split_axis=1, concat_axis=2, tiled=True)
    row_in_band = order_group * cycle_rows + jnp.arange(cycle_rows, dtype=jnp.int32)
    parity = (cycle_band * north_rows + row_in_band % north_rows) % 2
    weight_m = jnp.where(order_of_slot == 0, 1.0, 2.0).astype(jnp.float32)
    phase_turn = order_of_slot[None, :] * parity[:, None] % (2 * cycle_pixels)
    phase_angle = jnp.pi * phase_turn.astype(jnp.float32) / cycle_pixels
    cos_phase = jnp.cos(phase_angle)
    sin_phase = jnp.sin(phase_angle)
    spec_re = weight_m * (rows_fourier[0] * cos_phase - rows_fourier[1] * sin_phase)
    spec_im = weight_m * (rows_fourier[0] * sin_phase + rows_fourier[1] * cos_phase)
    full_re = jnp.zeros((cycle_rows, total_slots), jnp.float32).at[:, order_of_slot].set(spec_re)
    full_im = jnp.zeros((cycle_rows, total_slots), jnp.float32).at[:, order_of_slot].set(spec_im)
    tables = cycle_tables(total_slots, cycle_pixels)
    log_density = to_field(full_re, full_im, tables)
    inside = survey_mask.astype(jnp.float32)
    number = counts.astype(jnp.float32)
    weight = inside * jnp.exp(log_density)
    weight_total, count_total = lax.psum((jnp.sum(weight), jnp.sum(inside * number)), ("blk", "ma"))
    residual = inside * (number - count_total * weight / weight_total)
    modes_re, modes_im = from_field(residual, tables)
    picked_re = modes_re[:, order_of_slot]
    picked_im = modes_im[:, order_of_slot]
    back_re = weight_m * (picked_re * cos_phase + picked_im * sin_phase)
    back_im = weight_m * (picked_im * cos_phase - picked_re * sin_phase)
    backward = jnp.stack([back_re, back_im]).astype(jnp.bfloat16)
    rows_back = lax.all_to_all(backward, "ma", split_axis=2, concat_axis=1, tiled=True)
    rows_back = rows_back.reshape(4, north_rows, block_slots)
    table_block = legendre
    piece_sign = parity_signs(block_orders, degrees)
    summed = jnp.einsum("nsl,kns->skl", table_block, rows_back, preferred_element_type=jnp.float32)
    summed = summed.reshape(own_slots * lax.axis_size("blk"), 2, 2, degrees)
    combined = lax.psum_scatter(
        summed[:, :, 0] + piece_sign[:, None, :] * summed[:, :, 1],
        "blk",
        scatter_dimension=0,
        tiled=True,
    )
    return jnp.where(own_keep[:, None, :], amplitude[None, None, :] * combined, 0.0)


def solution(mesh):
    placed = (
        P(("ma", "blk"), None, None),
        P(),
        P("blk", "ma", None),
        P(),
        P(("blk", "ma"), None),
        P(("blk", "ma"), None),
    )
    return jax.shard_map(
        per_device,
        mesh=mesh,
        in_specs=placed,
        out_specs=P(("ma", "blk"), None, None),
        check_vma=False,
    )
```

profile of v0, /device:TPU:2, one launch (start us, length us, event | category | flops | bytes accessed | tf_op | source)
XLA Modules:
  0.0 1235.4 jit_solution(14530995837320122005)
XLA Ops:
  7.4 1.7 select_convert_fusion
  10.7 5.0 fusion.7
  15.6 98.5 %all-gather.2.cloned.1.call-done = bf16[640,2,2560]{2,1,0:T(2,128)(2,1)} async-done(((bf16[10,2,2560]{2,1,0:T(2,128)(2,1)}), bf16[640,2,2560]{2,1,0:T(2,128)(2,1)}) %all-gather.2.cloned.1.call-update) | async-done | bytes 6553616 | tf_op jit(solution)/shard_map/all_gather | solution.py:94
  114.1 11.5 broadcast_multiply_fusion
  125.7 20.8 %fusion.13 = f32[4,2,640]{0,1,2:T(2,128)S(1)} fusion(bf16[2,640,2560]{2,1,0:T(8,128)(2,1)} %param.8, bf16[640,2,2560]{2,1,0:T(2,128)(2,1)S(1)} %broadcast_multiply_fusion, bf16[640,2,2560]{2,1,0:T(2,128)(2,1)S(1)} %copy-done), kind=kOutput, calls=%fused_computation.24 | convolution fusion | flops 52428800 | bytes 19681280 | tf_op jit(solution)/shard_map/nsl,skl->kns/dot_general | solution.py:100
  147.4 5.4 all-to-all-start
  152.9 3.8 all-to-all-done
  157.0 9.9 scatter_custom_fusion
  167.5 9.9 scatter_custom_fusion.1
  180.1 74.5 %all-reduce.1 = (f32[]{:T(128)}, f32[]{:T(128)}) all-reduce(f32[]{:T(128)} %get-tuple-element.6, f32[]{:T(128)} %get-tuple-element.5), channel_id=1, replica_groups=mesh['blk'=64,'ma'=4] {'blk','ma'}, use_global_device_ids=true, to_apply=%region_5.6 | all-reduce | flops 2 | bytes 16 | tf_op jit(solution)/shard_map/psum | solution.py:123
  254.7 1.4 fusion.48
  258.5 13.6 %gather_fusion = f32[2560]{0:T(1024)S(1)} fusion(f32[2560]{0:T(1024)S(1)} %fusion.19, s32[3072]{0:T(1024)S(1)} %pad_clamp_fusion), kind=kCustom, calls=%fused_computation | custom fusion | bytes 30720 | tf_op jit(solution)/shard_map/gather | solution.py:126
  272.2 13.6 %gather_fusion.1 = f32[2560]{0:T(1024)S(1)} fusion(f32[2560]{0:T(1024)S(1)} %fusion.18, s32[3072]{0:T(1024)S(1)} %pad_clamp_fusion), kind=kCustom, calls=%fused_computation.1 | custom fusion | bytes 30720 | tf_op jit(solution)/shard_map/gather | solution.py:127
  285.9 1.1 copy.32
  287.5 14.3 %reduce.8 = bf16[2560,2]{1,0:T(8,128)(2,1)S(1)} reduce(bf16[2560,1,2]{2,1,0:T(2,128)(2,1)S(1)} %bitcast.51, bf16[]{:T(256)} %broadcast.237), dimensions={1}, to_apply=%bitcast.43.reduce_sub_computation | reduce | bytes 20482
  301.8 0.8 reshape.338
  302.6 6.8 all_to_all.8
  309.4 1.6 reshape.339
  312.0 25.5 %fusion.9 = f32[640,4,2560]{2,1,0:T(4,128)S(1)} fusion(bf16[4,2,640]{0,1,2:T(2,128)(2,1)S(1)} %copy.34, bf16[2,640,2560]{2,1,0:T(8,128)(2,1)} %param.8), kind=kOutput, calls=%fused_computation.19 | convolution fusion | flops 26214400 | bytes 32778240 | tf_op jit(solution)/shard_map/nsl,kns->skl/dot_general | solution.py:135
  337.5 15.9 %copy.36 = f32[640,4,2560]{2,0,1:T(8,128)} copy(f32[640,4,2560]{2,1,0:T(4,128)S(1)} %fusion.9) | data formatting | bytes 52428800 | tf_op jit(solution)/shard_map/nsl,kns->skl/dot_general | solution.py:135
  353.5 9.9 fusion.1
  363.4 25.2 %copy.38 = f32[640,2,2560]{2,1,0:T(2,128)} copy(f32[640,2,2560]{2,0,1:T(8,128)S(1)} %fusion.1) | data formatting | bytes 26214400 | tf_op jit(solution)/shard_map/add | solution.py:138
  390.5 836.3 %all-reduce.4.cloned.1.call-done = f32[640,2,2560]{2,1,0:T(2,128)} async-done(((f32[640,2,2560]{2,1,0:T(2,128)}), f32[640,2,2560]{2,1,0:T(2,128)}) %all-reduce.4.cloned.1.call-update) | async-done | bytes 13107216
  1226.8 1.8 fusion.20
  (58 shorter events, 12.0 us)
Async XLA Ops:
  6.5 107.6 %all-gather.2.cloned.1.call-start = ((), (), s32[]{:S(2)}) async-start(), calls=%async_computation.2 | async-start | bytes 6656000 | tf_op jit(solution)/shard_map/all_gather | solution.py:94
  114.1 11.5 copy-start
  125.7 31.1 %copy-start.1 = (s32[2560]{0:T(1024)S(1)}, s32[2560]{0:T(1024)}, u32[]{:S(2)}) copy-start(s32[2560]{0:T(1024)} %param.9) | copy-start | bytes 30724
  125.7 53.8 %copy-start.2 = (s32[1,8192]{1,0:T(1,128)S(1)}, s32[1,8192]{1,0:T(1,128)}, u32[]{:S(2)}) copy-start(s32[1,8192]{1,0:T(1,128)} %param.10) | copy-start | bytes 98308
  125.7 53.8 %copy-start.3 = (s32[1,8192]{1,0:T(1,128)S(1)}, s32[1,8192]{1,0:T(1,128)}, u32[]{:S(2)}) copy-start(s32[1,8192]{1,0:T(1,128)} %param.11) | copy-start | bytes 98308
  147.4 9.3 all-to-all-start
  152.8 1074.0 %all-reduce.4.cloned.1.call-start = ((), (), s32[]{:S(2)}) async-start(), calls=%async_computation.3 | async-start | bytes 26214400
  312.0 41.5 %slice-start = ((s8[6553600]{0:T(1024)(128)(4,1)}), s8[4194304]{0:T(1024)(128)(4,1)S(1)}, s32[]{:S(2)}) async-start(s8[6553600]{0:T(1024)(128)(4,1)} %bitcast.49), calls=%async_computation.4 | async-start | bytes 8388608
  337.5 16.0 %slice-start.1 = ((s8[6553600]{0:T(1024)(128)(4,1)}), s8[2359296]{0:T(1024)(128)(4,1)S(1)}, s32[]{:S(2)}) async-start(s8[6553600]{0:T(1024)(128)(4,1)} %bitcast.49), calls=%async_computation.5 | async-start | bytes 4718592
  388.6 0.7 copy-start.5
  388.6 838.2 %copy-start.4 = (f32[2560]{0:T(1024)S(1)}, f32[2560]{0:T(1024)}, u32[]{:S(2)}) copy-start(f32[2560]{0:T(1024)} %param.7) | copy-start | bytes 30724
Sparse Core Ops, SparseCore 0:
  10.7 103.3 all-gather.1
  388.7 838.0 all-reduce.3
where the time goes:
time: 1240 us
  waiting for transfers between devices  939 us (76%)
  local copies, waits for them, and re-layouts  97.2 us (8%)
  blocking collectives  81.3 us (7%)
  matrix products  51 us (4%)
  other arithmetic  47.4 us (4%)
  between operations  14.4 us (1%)
    unnamed x3, waiting for transfers between devices  836 us
    all_gather x1, waiting for transfers between devices, per_device(): shard_rows = lax.all_gather(harmonics, 'blk', axis=0, tiled=True)  98.5 us
    psum x1, blocking collectives, per_device(): lax.psum((jnp.sum(weight), jnp.sum(inside * number)), ('blk', 'ma'))  74.5 us
    dot_general x1, matrix products, per_device(): jnp.einsum('nsl,kns->skl', table_block, rows_back, preferred_element_type...  25.5 us
    add x1, local copies, waits for them, and re-layouts, per_device(): summed[:, :, 0] + piece_sign[:, None, :] * summed[:, :, 1]  25.2 us
  transfers between devices with their start and end apart: 3, of which 3 were waited for; matrix products, arithmetic and copies ran while one was open for 1% of the time, Pallas kernels for 0%

commit v1 on v0

v1 whole, which is shorter than its diff:
```python
import functools

import jax
import jax.numpy as jnp
import numpy as np
from jax import lax
from jax.experimental import pallas as pl
from jax.experimental.pallas import tpu as pltpu
from jax.sharding import PartitionSpec as P

MESH = pl.DeviceIdType.MESH
F32 = jnp.float32
BF16 = jnp.bfloat16
EXACT = lax.Precision.HIGHEST

SIDE = 4
OWN = 5
PAIRS = 80
XT, YT = 11, 10
LANES = (XT * 128, YT * 128)


def nt(a, b, precision=None):
    return lax.dot_general(
        a, b, (((1,), (1,)), ((), ())), preferred_element_type=F32, precision=precision
    )


def nn(a, b, precision=None):
    return lax.dot_general(
        a, b, (((1,), (0,)), ((), ())), preferred_element_type=F32, precision=precision
    )


def selection_tables():
    pick_x = np.zeros((2, 160, 192), np.float32)
    for odd in range(2):
        for y in range(SIDE):
            for i in range(20):
                for ab in range(2):
                    pick_x[odd, ab * 80 + y * 20 + i, y * 48 + odd * 8 + 2 * i + ab] = 1
    pick_y = np.zeros((160, 160), np.float32)
    for i in range(80):
        for ab in range(2):
            pick_y[ab * 80 + i, 2 * i + ab] = 1
    flip = np.fliplr(np.eye(256, dtype=np.float32))
    spread = np.zeros((512, 480), np.float32)
    for dev in range(16):
        for j in range(3):
            for c in range(2):
                for k in range(OWN):
                    spread[dev * 32 + (j * 2 + c) * OWN + k, (j * 2 + c) * 80 + dev * OWN + k] = 1
    alt = np.where(np.arange(128) % 2 == 0, 1.0, -1.0)
    expand = np.zeros((32, 1024), np.float32)
    for r in range(4):
        for e in range(4):
            col = ((r % 2) * 4 + e) * 128
            expand[r * 8 + e, col : col + 128] = 1.0 if r < 2 else alt
    lane_sum = np.zeros((8, 128), np.float32)
    lane_sum[0] = 1
    lane_sum[1] = alt
    eye = np.eye(128, dtype=np.float32)
    return [
        np.asarray(t, jnp.bfloat16)
        for t in (pick_x, pick_y, flip, spread, spread.T.copy(), expand, lane_sum, eye)
    ]


def dft_tables():
    p = np.arange(40)
    q = np.arange(64)
    u = np.arange(64)
    v = np.arange(128)
    synth, turn_a, turn_b, back_re, back_im, gather = [], [], [], [], [], []
    for h in range(2):
        coarse = 2 * np.pi * ((p[:, None] * (2 * v[None, :] + h)) % 256) / 256
        c, s = np.cos(coarse), np.sin(coarse)
        top = np.concatenate([c.T, -s.T], 1)
        low = np.concatenate([s.T, c.T], 1)
        synth.append(np.concatenate([top, low], 0))
        turn = 2 * np.pi * ((q[None, :] * (2 * v[:, None] + h)) % 16384) / 16384
        tc, ts = np.cos(turn), np.sin(turn)
        turn_a.append(np.concatenate([tc, ts], 1))
        turn_b.append(np.concatenate([-ts, tc], 1))
        back_re.append(tc.T.copy())
        back_im.append(ts.T.copy())
        gather.append(
            np.concatenate([np.concatenate([c, s], 1), np.concatenate([-s, c], 1)], 0)
        )
    fine = 2 * np.pi * ((q[None, :] * u[:, None]) % 64) / 64
    fc, fs = np.cos(fine), np.sin(fine)
    fine_out = np.concatenate([fc, -fs], 1)
    fine_in = np.concatenate([fc.T, -fs.T], 0)
    weight = np.full((80, 128), 2.0)
    weight[0, 0] = weight[40, 0] = weight[0, 64] = weight[40, 64] = 1.0
    return [
        np.asarray(t, np.float32)
        for t in (
            np.stack(synth),
            np.stack(turn_a),
            np.stack(turn_b),
            np.stack(back_re),
            np.stack(back_im),
            np.stack(gather),
            fine_out,
            fine_in,
            weight,
        )
    ]


def kernel(
    leg, harm, thr, ordv, cnt, msk,
    pick_x, pick_y, flip, spread, spread_t, expand, lane_sum, eye,
    synth, turn_a, turn_b, back_re, back_im, gather, fine_out, fine_in, weight,
    out,
    lg, ls_x, ls_y, lr_x, lr_y, hg1, hg, hst, accs, fsend, frecv, pt, qt,
    bsend, brecv, psend, precv, coef, gst, gs1, gr1, gs2, gr2,
    lg_sem, ls_sem, lrecv_sem, h1s, h1r, h2s, h2r, fs_sem, fr_sem, bs_sem, br_sem,
    ps_sem, pr_sem, g1s, g1r, g2s, g2r,
):
    b = lax.axis_index("blk")
    g = lax.axis_index("ma")
    y, x, z = b // 16, (b // 4) % 4, b % 4
    pending = []

    def at(yy, xx, zz, gg):
        return (yy * 16 + xx * 4 + zz, gg)

    def shift(v, d):
        return lax.rem(v + d, 4) if d else v

    def remote(src, dst, ssem, rsem, dev):
        return pltpu.make_async_remote_copy(
            src_ref=src, dst_ref=dst, send_sem=ssem, recv_sem=rsem, device_id=dev, device_id_type=MESH
        )

    def send(src, dst, ssem, rsem, dev):
        c = remote(src, dst, ssem, rsem, dev)
        c.start()
        pending.append(c)

    peers = []
    for dx in range(4):
        for dg in range(4):
            if dx or dg:
                peers.append((0, dx, 0, dg))
    for dy in range(1, 4):
        for dg in range(4):
            peers.append((dy, 0, 0, dg))
    for dy in range(4):
        for dz in range(1, 4):
            peers.append((dy, 0, dz, 0))
    barrier = pltpu.get_barrier_semaphore()
    for dy, dx, dz, dg in peers:
        pl.semaphore_signal(
            barrier, inc=1, device_id=at(shift(y, dy), shift(x, dx), shift(z, dz), shift(g, dg)),
            device_id_type=MESH,
        )

    order = (1, 3, 2, 0)
    loads = {}
    for d in order:
        yy = shift(y, d)
        rows = pl.ds(pl.multiple_of(yy * 160, 32), 160)
        for n in range(2):
            c = pltpu.make_async_copy(leg.at[n, rows], lg.at[n, rows], lg_sem.at[n, d])
            c.start()
            loads[d, n] = c

    accs[...] = jnp.zeros_like(accs)
    gst[...] = jnp.zeros_like(gst)

    pl.semaphore_wait(barrier, len(peers))

    for m in range(2):
        hg1[m, z] = harm[m]
    for d in (1, 3, 2):
        send(harm, hg1.at[:, z], h1s.at[d], h1r.at[z], at(y, x, shift(z, d), g))

    def pack(mode, dest, n):
        t_all = thr[mode, dest]
        wide = jnp.concatenate([t_all, t_all - 128], axis=1)
        if mode == 0:
            start = (dest // 2) * 80 + (dest % 2) * 32
            sel = pick_x[dest % 2]
            buf = ls_x.at[dest, n]

            def columns(c0, width):
                return jnp.concatenate(
                    [
                        lg[n, pl.ds(pl.multiple_of(k * 160 + start, 16), 48), c0 : c0 + width]
                        for k in range(4)
                    ],
                    axis=0,
                )
        else:
            sel = pick_y[...]
            buf = ls_y.at[dest, n]

            def columns(c0, width):
                return lg[n, pl.ds(pl.multiple_of(dest * 160, 32), 160), c0 : c0 + width]

        even, odd = sel[0:80], sel[80:160]

        def a_part(tile, tiles):
            return nn(even, columns(tile * 128, tiles * 128))

        def b_part(tile, tiles):
            part = nn(odd, columns(tile * 128, tiles * 128)).astype(BF16)
            f = flip[...] if tiles == 2 else flip[128:256, 0:128]
            return nn(part, f)

        first, last = (0, XT) if mode == 0 else (XT, XT + YT)
        t = first
        while t < last:
            o = (t - first) * 128
            if t == 0:
                buf[:, o : o + 128] = b_part(19, 1).astype(BF16)
                t += 1
            elif t == 19:
                mix = jnp.where(t_all <= 128 * t, a_part(t - 1, 1), b_part(0, 1))
                buf[:, o : o + 128] = mix.astype(BF16)
                buf[:, o + 128 : o + 256] = a_part(t, 1).astype(BF16)
                t += 2
            else:
                mix = jnp.where(wide <= 128 * t, a_part(t - 1, 2), b_part(18 - t, 2))
                buf[:, o : o + 256] = mix.astype(BF16)
                t += 2

    send_bufs, recv_bufs = (ls_x, ls_y), (lr_x, lr_y)

    def place(mode, other, r):
        return at(y, other, z, r) if mode == 0 else at(other, x, z, r)

    def mine(mode):
        return x if mode == 0 else y

    def exchange(mode, d):
        dest = shift(mine(mode), d)
        for n in range(2):
            pack(mode, dest, n)
            src, dst = send_bufs[mode].at[dest, n], recv_bufs[mode].at[mine(mode), n]
            if d:
                send(src, dst, ls_sem.at[mode, d, n], lrecv_sem.at[mode, mine(mode), n], place(mode, dest, g))
            else:
                recv_bufs[mode][mine(mode), n] = send_bufs[mode][dest, n]

    for step, d in enumerate(order):
        if step == 0:
            for n in range(2):
                loads[d, n].wait()
        exchange(1, d)
        if step == 0:
            for dd in order[1:]:
                for n in range(2):
                    loads[dd, n].wait()
        exchange(0, d)
        if step == 0:
            for dd in (1, 3, 2):
                zz = shift(z, dd)
                remote(harm, hg1.at[:, zz], h1s.at[dd], h1r.at[zz], at(y, x, zz, g)).wait_recv()
            for m in range(2):
                hg[m, y if m == 0 else x] = hg1[m]
                for dd in (1, 3, 2):
                    who = at(shift(y, dd), x, z, g) if m == 0 else at(y, shift(x, dd), z, g)
                    me = y if m == 0 else x
                    send(hg1.at[m], hg.at[m, me], h2s.at[m, dd], h2r.at[m, me], who)

    def digits(i, carry):
        o = ordv[i]
        row = jnp.concatenate([o[0:1], o[1:2]], axis=1)
        hi = row >> 6
        lo = row & 63
        pt[i] = jnp.where(
            lax.broadcasted_iota(jnp.int32, (40, 256), 0) == hi, 1.0, 0.0
        ).astype(F32)
        qt[i] = jnp.where(
            (lax.broadcasted_iota(jnp.int32, (128, 256), 0) & 63) == lo, 1.0, 0.0
        ).astype(BF16)
        return carry

    lax.fori_loop(0, 32, digits, 0)

    for m in range(2):
        for dd in (1, 3, 2):
            me = shift(y if m == 0 else x, dd)
            remote(hg1.at[m], hg.at[m, me], h2s.at[m, dd], h2r.at[m, me], at(y, x, z, g)).wait_recv()
        blocks = hg[m].reshape(512, 512)

        def unstack(i, carry):
            rows = pl.ds(pl.multiple_of(i * 80, 16), 80)
            hst[m, rows, :] = nn(spread_t[rows, :], blocks)
            return carry

        lax.fori_loop(0, 6, unstack, 0)

    def synthesize(mode, src):
        tiles = (XT, YT)[mode]
        table = recv_bufs[mode]
        own = mine(mode)

        def group(i, carry):
            r0 = pl.multiple_of(i * 16, 16)
            rows = pl.ds(r0, 16)
            limit = thr[mode, own, rows, :]
            total = [[None, None], [None, None]]
            upper = [[None, None], [None, None]]
            for t in range(tiles):
                tile = t + (0 if mode == 0 else XT)
                is_a = limit <= 128 * tile
                for c in range(2):
                    row = pl.ds(pl.multiple_of(((t // 4) * 2 + c) * 80 + r0, 16), 16)
                    h = hst[mode, row, (t % 4) * 128 : (t % 4) * 128 + 128]
                    for n in range(2):
                        v = table[src, n, rows, t * 128 : t * 128 + 128].astype(F32) * h
                        w = jnp.where(is_a, v, 0.0)
                        total[n][c] = v if t == 0 else total[n][c] + v
                        upper[n][c] = w if t == 0 else upper[n][c] + w
            for n in range(2):
                for c in range(2):
                    accs[n, 2 * c, rows, :] = upper[n][c]
                    accs[n, 2 * c + 1, rows, :] = total[n][c] - upper[n][c]
            return carry

        lax.fori_loop(0, 5, group, 0)
        sign = jnp.where((ordv[mode * 16 + own * 4 + g, 0:1, :] & 1) == 1, -1.0, 1.0)
        signs = jnp.concatenate([sign] * 4, axis=1)
        for n in range(2):
            rows = accs[n].reshape(512, 128)
            hi = rows.astype(BF16)
            lo = (rows - hi.astype(F32)).astype(BF16)
            both = nt(lane_sum[...], hi) + nt(lane_sum[...], lo)
            fsend[mode, src, n] = both[0:1]
            fsend[mode, src, n + 2] = both[1:2] * signs

    for step, d in enumerate((0, 3, 1, 2)):
        for mode in (1, 0):
            own = mine(mode)
            src = shift(own, d)
            if d:
                for n in range(2):
                    remote(
                        send_bufs[mode].at[src, n], recv_bufs[mode].at[src, n],
                        ls_sem.at[mode, d, n], lrecv_sem.at[mode, src, n], at(y, x, z, g),
                    ).wait_recv()
            synthesize(mode, src)
            for e in range(4):
                r = shift(g, e)
                if d or e:
                    send(
                        fsend.at[mode, src, r], frecv.at[mode, own, g],
                        fs_sem.at[mode, d, e], fr_sem.at[mode, own, g], place(mode, src, r),
                    )
                else:
                    frecv[mode, own, g] = fsend[mode, src, r]

    for mode in (1, 0):
        for d in range(4):
            for e in range(4):
                if d or e:
                    p, r = shift(mine(mode), d), shift(g, e)
                    remote(
                        fsend.at[mode, p, r], frecv.at[mode, p, r],
                        fs_sem.at[mode, d, e], fr_sem.at[mode, p, r], at(y, x, z, g),
                    ).wait_recv()

    h = g % 2

    def scatter(i, total):
        row = frecv[i // 16, (i // 4) % 4, i % 4]
        digit = pt[i]
        both = jnp.concatenate([digit * row[:, 0:256], digit * row[:, 256:512]], axis=0)
        hi = both.astype(BF16)
        lo = (both - hi.astype(F32)).astype(BF16)
        return total + nt(jnp.concatenate([hi, lo], axis=0), qt[i])

    full = lax.fori_loop(0, 32, scatter, jnp.zeros((160, 128), F32))
    full = (full[0:80] + full[80:160]) * weight[...]
    section = nn(synth[h], full, EXACT)
    turned = section[0:128] * turn_a[h] + section[128:256] * turn_b[h]
    log_density = nt(fine_out[...], turned, EXACT)
    inside = msk[...].astype(F32)
    number = inside * cnt[...].astype(F32)
    dens = inside * jnp.exp(log_density)
    psend[0, 0] = jnp.concatenate(
        [jnp.sum(dens, axis=0, keepdims=True), jnp.sum(number, axis=0, keepdims=True)], axis=1
    )
    precv[0, x, g] = psend[0, 0]
    for d in range(4):
        for e in range(4):
            if d or e:
                send(
                    psend.at[0, 0], precv.at[0, x, g], ps_sem.at[0, d, e], pr_sem.at[0, x, g],
                    at(y, shift(x, d), z, shift(g, e)),
                )

    first = nn(fine_in[...], jnp.concatenate([number, dens], axis=1), EXACT)
    modes = []
    for f in range(2):
        re, im = first[0:64, f * 128 : f * 128 + 128], first[64:128, f * 128 : f * 128 + 128]
        tre = re * back_re[h] + im * back_im[h]
        tim = im * back_re[h] - re * back_im[h]
        both = jnp.concatenate([tre, tim], axis=1)
        modes.append(nt(gather[h], jnp.concatenate([both, both], axis=0), EXACT) * weight[...])
    modes = jnp.concatenate(modes, axis=0)
    modes_hi = modes.astype(BF16).astype(F32)
    lane = lax.broadcasted_iota(jnp.int32, (160, 128), 1)
    modes = jnp.where(lane < 64, modes_hi, modes - modes_hi).astype(BF16)

    for d in range(4):
        for e in range(4):
            if d or e:
                xx, gg = shift(x, d), shift(g, e)
                remote(
                    psend.at[0, 0], precv.at[0, xx, gg], ps_sem.at[0, d, e], pr_sem.at[0, xx, gg],
                    at(y, x, z, g),
                ).wait_recv()
    psend[1, 0] = jnp.sum(precv[0].reshape(16, 1, 256), axis=0)
    precv[1, y, z] = psend[1, 0]
    for d in range(4):
        for e in range(4):
            if d or e:
                send(
                    psend.at[1, 0], precv.at[1, y, z], ps_sem.at[1, d, e], pr_sem.at[1, y, z],
                    at(shift(y, d), x, shift(z, e), g),
                )

    def picks(i, carry):
        rows = nn(modes, qt[i])
        digit = pt[i]
        for k in range(4):
            line = jnp.sum(rows[k * 40 : k * 40 + 40] * digit, axis=0, keepdims=True)
            for ab in range(2):
                bsend[i // 16, (i // 4) % 4, i % 4, 2 * k + ab : 2 * k + ab + 1, :] = line[
                    :, ab * 128 : ab * 128 + 128
                ]
        return carry

    lax.fori_loop(0, 32, picks, 0)

    for mode in (1, 0):
        own = mine(mode)
        for d in range(4):
            for e in range(4):
                p, gg = shift(own, d), shift(g, e)
                if d or e:
                    send(
                        bsend.at[mode, p, gg], brecv.at[mode, own, g],
                        bs_sem.at[mode, d, e], br_sem.at[mode, own, g], place(mode, p, gg),
                    )
                else:
                    brecv[mode, own, g] = bsend[mode, p, gg]

    for d in range(4):
        for e in range(4):
            if d or e:
                yy, zz = shift(y, d), shift(z, e)
                remote(
                    psend.at[1, 0], precv.at[1, yy, zz], ps_sem.at[1, d, e], pr_sem.at[1, yy, zz],
                    at(y, x, z, g),
                ).wait_recv()
    sums = jnp.sum(precv[1].reshape(16, 1, 256), axis=0)
    ratio = jnp.sum(sums[:, 128:256], axis=1, keepdims=True) / jnp.sum(
        sums[:, 0:128], axis=1, keepdims=True
    )

    def analyse(mode):
        tiles = (XT, YT)[mode]
        own = mine(mode)
        for d in range(4):
            for e in range(4):
                if d or e:
                    p, r = shift(own, d), shift(g, e)
                    remote(
                        bsend.at[mode, p, r], brecv.at[mode, p, r],
                        bs_sem.at[mode, d, e], br_sem.at[mode, p, r], at(y, x, z, g),
                    ).wait_recv()
        sign = jnp.where((ordv[mode * 16 + own * 4 + g, 0:1, :] & 1) == 1, -1.0, 1.0)
        for p in range(4):
            lines = []
            for r in range(4):
                tile = brecv[mode, p, r]
                line = tile - ratio * pltpu.roll(tile, 4, 0)
                line = jnp.where(lax.broadcasted_iota(jnp.int32, (8, 128), 0) < 4, line, 0.0)
                lines.append(line if r < 2 else line * sign)
            across = nt(eye[...], jnp.concatenate(lines, axis=0).astype(BF16))
            coef[p] = nn(across[0:80].astype(BF16), expand[...])
        table = recv_bufs[mode]

        def group(i, carry):
            r0 = pl.multiple_of(i * 16, 16)
            rows = pl.ds(r0, 16)
            limit = thr[mode, own, rows, :]
            for c in range(2):
                co = [
                    [
                        [coef[p, rows, ((n * 2 + c) * 2 + ab) * 128 : ((n * 2 + c) * 2 + ab) * 128 + 128] for ab in range(2)]
                        for n in range(2)
                    ]
                    for p in range(4)
                ]
                for t in range(tiles):
                    is_a = limit <= 128 * (t + (0 if mode == 0 else XT))
                    total = None
                    for p in range(4):
                        for n in range(2):
                            v = table[p, n, rows, t * 128 : t * 128 + 128].astype(F32) * jnp.where(
                                is_a, co[p][n][0], co[p][n][1]
                            )
                            total = v if total is None else total + v
                    row = pl.ds(pl.multiple_of(((t // 4) * 2 + c) * 80 + r0, 16), 16)
                    gst[mode, row, (t % 4) * 128 : (t % 4) * 128 + 128] = total.astype(BF16)
            return carry

        lax.fori_loop(0, 5, group, 0)
        across = y if mode == 0 else x
        for d in (1, 3, 2, 0):
            dest = shift(across, d)
            rows = pl.ds(pl.multiple_of(dest * 128, 128), 128)
            part = nn(spread[rows, :], gst[mode]).astype(BF16)
            if d:
                gs1[mode, dest] = part
                who = at(dest, x, z, g) if mode == 0 else at(y, dest, z, g)
                send(gs1.at[mode, dest], gr1.at[mode, across], g1s.at[mode, d], g1r.at[mode, across], who)
            else:
                gr1[mode, across] = part

    for mode in (1, 0):
        analyse(mode)

    for mode in (1, 0):
        across = y if mode == 0 else x
        for d in (1, 3, 2):
            src = shift(across, d)
            remote(gs1.at[mode, src], gr1.at[mode, src], g1s.at[mode, d], g1r.at[mode, src], at(y, x, z, g)).wait_recv()
        total = gr1[mode, 0].astype(F32)
        for k in range(1, 4):
            total = total + gr1[mode, k].astype(F32)
        gs2[mode] = total.astype(BF16).reshape(4, 32, 512)
        gr2[mode, z] = gs2[mode, z]
        for d in (1, 3, 2):
            dest = shift(z, d)
            send(gs2.at[mode, dest], gr2.at[mode, z], g2s.at[mode, d], g2r.at[mode, z], at(y, x, dest, g))
    for mode in (1, 0):
        for d in (1, 3, 2):
            src = shift(z, d)
            remote(gs2.at[mode, src], gr2.at[mode, src], g2s.at[mode, d], g2r.at[mode, src], at(y, x, z, g)).wait_recv()
        total = gr2[mode, 0].astype(F32)
        for k in range(1, 4):
            total = total + gr2[mode, k].astype(F32)
        out[mode] = total

    for c in pending:
        c.wait_send()


def per_device(white_noise, amplitude, legendre, order_of_slot, counts, survey_mask):
    blk = lax.axis_index("blk")
    ma = lax.axis_index("ma")
    degrees = legendre.shape[2]
    own_slots = white_noise.shape[0]
    bands = lax.axis_size("blk")
    own_orders = lax.dynamic_slice_in_dim(order_of_slot, (ma * bands + blk) * own_slots, own_slots)
    degree = jnp.arange(degrees, dtype=jnp.int32)
    own_keep = degree[None, :] >= own_orders[:, None]
    harmonics = jnp.where(own_keep[:, None, :], amplitude[None, None, :] * white_noise, 0.0).astype(BF16)
    pairs = harmonics.reshape(OWN, 2, 2, degrees)
    line = jnp.pad(pairs[:, 0], ((0, 0), (0, 0), (128, 0))) + jnp.pad(
        pairs[:, 1, :, ::-1], ((0, 0), (0, 0), (0, 128))
    )
    halves = []
    for lo, hi in ((0, LANES[0]), (LANES[0], LANES[0] + LANES[1])):
        part = jnp.pad(line[:, :, lo:hi], ((0, 0), (0, 0), (0, 1536 - (hi - lo))))
        part = part.reshape(OWN, 2, 3, 512).transpose(2, 1, 0, 3).reshape(30, 512)
        halves.append(jnp.pad(part, ((0, 2), (0, 0))))
    harm = jnp.stack(halves)

    grid = order_of_slot.reshape(4, 4, 4, 20, 2)
    by_x = grid.transpose(2, 0, 4, 1, 3).reshape(4, 4, 2, 80)
    by_y = grid.transpose(1, 0, 4, 2, 3).reshape(4, 4, 2, 80)
    ordv = jnp.stack([by_x, by_y])
    own_even = lax.dynamic_index_in_dim(ordv[:, :, :, 0], ma, axis=2, keepdims=False)
    thr = own_even[..., None] + 128 - jnp.arange(128, dtype=jnp.int32)
    ordv = jnp.pad(ordv, ((0, 0),) * 4 + ((0, 48),), constant_values=-1).reshape(32, 2, 128)

    tables = [jnp.asarray(t) for t in selection_tables() + dft_tables()]
    vmem = pl.BlockSpec(memory_space=pltpu.VMEM)
    dma = pltpu.SemaphoreType.DMA
    got = pl.pallas_call(
        kernel,
        out_shape=jax.ShapeDtypeStruct((2, 32, 512), F32),
        in_specs=[pl.BlockSpec(memory_space=pl.ANY)] + [vmem] * (5 + len(tables)),
        out_specs=vmem,
        scratch_shapes=[
            pltpu.VMEM((2, 640, 2560), BF16),
            pltpu.VMEM((4, 2, 80, LANES[0]), BF16),
            pltpu.VMEM((4, 2, 80, LANES[1]), BF16),
            pltpu.VMEM((4, 2, 80, LANES[0]), BF16),
            pltpu.VMEM((4, 2, 80, LANES[1]), BF16),
            pltpu.VMEM((2, 4, 32, 512), BF16),
            pltpu.VMEM((2, 4, 4, 32, 512), BF16),
            pltpu.VMEM((2, 480, 512), F32),
            pltpu.VMEM((2, 4, 128, 128), F32),
            pltpu.VMEM((2, 4, 4, 1, 512), F32),
            pltpu.VMEM((2, 4, 4, 1, 512), F32),
            pltpu.VMEM((32, 40, 256), F32),
            pltpu.VMEM((32, 128, 256), BF16),
            pltpu.VMEM((2, 4, 4, 8, 128), F32),
            pltpu.VMEM((2, 4, 4, 8, 128), F32),
            pltpu.VMEM((2, 1, 1, 256), F32),
            pltpu.VMEM((2, 4, 4, 1, 256), F32),
            pltpu.VMEM((4, 80, 1024), F32),
            pltpu.VMEM((2, 480, 512), BF16),
            pltpu.VMEM((2, 4, 128, 512), BF16),
            pltpu.VMEM((2, 4, 128, 512), BF16),
            pltpu.VMEM((2, 4, 32, 512), BF16),
            pltpu.VMEM((2, 4, 32, 512), BF16),
            dma((2, 4)),
            dma((2, 4, 2)),
            dma((2, 4, 2)),
            dma((4,)),
            dma((4,)),
            dma((2, 4)),
            dma((2, 4)),
            dma((2, 4, 4)),
            dma((2, 4, 4)),
            dma((2, 4, 4)),
            dma((2, 4, 4)),
            dma((2, 4, 4)),
            dma((2, 4, 4)),
            dma((2, 4)),
            dma((2, 4)),
            dma((2, 4)),
            dma((2, 4)),
        ],
        compiler_params=pltpu.CompilerParams(
            collective_id=0, has_side_effects=True, vmem_limit_bytes=50 * 1024 * 1024
        ),
        name="survey",
    )(
        legendre, harm, thr, ordv, counts.reshape(64, 128), survey_mask.reshape(64, 128), *tables
    )
    lines = got[:, :30].reshape(2, 3, 2, OWN, 512).transpose(0, 3, 2, 1, 4).reshape(2, OWN, 2, 1536)
    line = jnp.concatenate([lines[0, :, :, : LANES[0]], lines[1, :, :, : LANES[1]]], axis=2)
    summed = jnp.stack([line[:, :, 128:], line[:, :, degrees - 1 :: -1]], axis=1)
    summed = summed.reshape(own_slots, 2, degrees)
    return jnp.where(own_keep[:, None, :], amplitude[None, None, :] * summed, 0.0)


def solution(mesh):
    placed = (
        P(("ma", "blk"), None, None),
        P(),
        P("blk", "ma", None),
        P(),
        P(("blk", "ma"), None),
        P(("blk", "ma"), None),
    )
    return jax.shard_map(
        per_device,
        mesh=mesh,
        in_specs=placed,
        out_specs=P(("ma", "blk"), None, None),
        check_vma=False,
    )
```

time: 1240 us -> 120 us (0.10)
  waiting for transfers between devices: 939 us -> 0 us
  Pallas kernels: 0 us -> 91.8 us
  blocking collectives: 81.3 us -> 0 us
  local copies, waits for them, and re-layouts: 97.2 us -> 23.7 us
  matrix products: 51 us -> 0 us
  other arithmetic: 47.4 us -> 3.16 us
  between operations: 14.4 us -> 0.27 us
    unnamed x3 -> x0, waiting for transfers between devices: 836 us -> none
    all_gather x1 -> x0, waiting for transfers between devices: 98.5 us -> none  [per_device(): shard_rows = lax.all_gather(harmonics, 'blk', axis=0, tiled=True)]
    pallas_call x0 -> x1, Pallas kernels: none -> 91.8 us  [per_device(): pl.pallas_call(kernel, out_shape=jax.ShapeDtypeStruct((2, 32, 512), F32),...]
    psum x1 -> x0, blocking collectives: 74.5 us -> none  [per_device(): lax.psum((jnp.sum(weight), jnp.sum(inside * number)), ('blk', 'ma'))]
    dot_general x14 -> x0, matrix products: 51 us -> none  [the longest x1 25.5 us: per_device(): jnp.einsum('nsl,kns->skl', table_block, rows_back, preferred_element_type...]
    gather x2 -> x0, local copies, waits for them, and re-layouts: 27.2 us -> none  [the longest x1 13.6 us: per_device(): picked_re = modes_re[:, order_of_slot]]
    add x1 -> x0, local copies, waits for them, and re-layouts: 25.2 us -> none  [per_device(): summed[:, :, 0] + piece_sign[:, None, :] * summed[:, :, 1]]
    scatter x2 -> x0, local copies, waits for them, and re-layouts: 19.9 us -> none  [per_device(): jnp.zeros((cycle_rows, total_slots), jnp.float32).at[:, order_of_slot]]
  transfers between devices with their start and end apart: 3 -> 0, of which waited for: 3 -> 0; matrix products, arithmetic and copies ran while one was open for 1% -> 0% of each run, Pallas kernels for 0% -> 0%
where the time goes in v1:
time: 120 us; the launch traced here: 119 us
  Pallas kernels  91.8 us (76%)
  local copies, waits for them, and re-layouts  23.7 us (20%)
  other arithmetic  3.16 us (3%)
    pallas_call x1, Pallas kernels, per_device(): pl.pallas_call(kernel, out_shape=jax.ShapeDtypeStruct((2, 32, 512), F32),...  91.8 us
    unnamed x41, local copies, waits for them, and re-layouts  16.3 us

profile of v1, /device:TPU:2, one launch (start us, length us, event | category | flops | bytes accessed | tf_op | source)
XLA Modules:
  0.0 118.9 jit_solution(15985831024914604359)
XLA Ops:
  0.0 0.8 dynamic_slice.7
  0.9 1.1 select_convert_fusion
  2.0 2.0 %rev.6 = bf16[5,1,2,2560]{3,2,0,1:T(2,128)(2,1)S(1)} reverse(bf16[5,1,2,2560]{3,2,0,1:T(2,128)(2,1)S(1)} %get-tuple-element.8), dimensions={3} | reverse | bytes 102400 | tf_op jit(solution)/shard_map/rev | solution.py:570
  5.1 1.0 reshape.71
  7.5 1.0 copy-done
  8.5 1.0 copy-done.1
  9.6 0.9 copy-done.2
  10.5 0.9 copy-done.3
  11.4 0.9 copy-done.4
  12.3 0.9 copy-done.5
  13.2 0.9 copy-done.6
  14.2 0.9 copy-done.7
  15.1 0.9 copy-done.8
  15.9 0.8 copy-done.9
  16.8 0.8 copy-done.10
  17.6 0.8 copy-done.11
  18.5 0.8 copy-done.12
  19.3 0.8 copy-done.13
  20.1 0.8 copy-done.14
  20.8 0.8 copy-done.15
  21.6 0.8 copy-done.16
  23.8 91.8 %survey.1 = f32[2,32,512]{2,1,0:T(8,128)S(1)} custom-call(bf16[2,640,2560]{2,1,0:T(8,128)(2,1)} %leg.1, bf16[2,32,512]{2,1,0:T(8,128)(2,1)S(1)} %pad_maximum_fusion.2.harm, s32[2,4,80,128]{3,2,1,0:T(8,128)S(1)} %iota_subtract_fusion.thr, s32[32,2,128]{2,1,0:T(2,128)S(1)} %bitcast.36, s32[64,128]{1,0:T(8,128)S(1)} %bitcast.37, s32[64,128]{1,0:T(8,128)S(1)} %bitcast.38, ...), custom_call_target="tpu_custom_call" | custom-call | tf_op jit(solution)/shard_map/survey/pallas_call | solution.py:590
  116.0 1.9 %rev.7 = f32[5,2,2560]{2,1,0:T(2,128)S(1)} reverse(f32[5,2,2560]{2,1,0:T(2,128)S(1)} %get-tuple-element.6), dimensions={2} | reverse | bytes 204800 | tf_op jit(solution)/shard_map/rev | solution.py:646
  118.1 0.8 fusion
  (54 shorter events, 4.5 us)
Async XLA Ops:
  6.6 111.4 %copy-start.19 = (f32[2560]{0:T(1024)S(1)}, f32[2560]{0:T(1024)}, u32[]{:S(2)}) copy-start(f32[2560]{0:T(1024)} %param.24) | copy-start | bytes 30724
  7.5 1.0 copy-start
  8.5 1.0 copy-start.1
  9.6 0.9 copy-start.2
  10.5 0.9 copy-start.3
  11.4 0.9 copy-start.4
  12.3 0.9 copy-start.5
  13.2 0.9 copy-start.6
  14.2 0.9 copy-start.7
  15.1 0.9 copy-start.8
  15.9 0.8 copy-start.9
  16.8 0.8 copy-start.10
  17.6 0.8 copy-start.11
  18.5 0.8 copy-start.12
  19.3 0.8 copy-start.13
  20.1 0.8 copy-start.14
  20.8 0.8 copy-start.15
  21.6 0.8 copy-start.16
  22.4 0.8 copy-start.17
  23.1 0.7 copy-start.18

commit v2 on v1

v2 whole, which is shorter than its diff:
```python
import functools

import jax
import jax.numpy as jnp
import numpy as np
from jax import lax
from jax.experimental import pallas as pl
from jax.experimental.pallas import tpu as pltpu
from jax.sharding import PartitionSpec as P

MESH = pl.DeviceIdType.MESH
F32 = jnp.float32
BF16 = jnp.bfloat16

SIDE = 4
OWN = 5
PAIRS = 80
XT, YT = 12, 9
PIECE = (XT // 3, YT // 3)
LANES = (XT * 128, YT * 128)


def nt(a, b):
    return lax.dot_general(
        a, b, (((1,), (1,)), ((), ())), preferred_element_type=F32
    )


def nn(a, b):
    return lax.dot_general(
        a, b, (((1,), (0,)), ((), ())), preferred_element_type=F32
    )


def selection_tables():
    flip = np.fliplr(np.eye(256, dtype=np.float32))
    spread = np.zeros((512, 480), np.float32)
    for dev in range(16):
        for j in range(3):
            for c in range(2):
                for k in range(OWN):
                    spread[dev * 32 + j * 10 + 2 * k + c, (j * 2 + c) * 80 + dev * OWN + k] = 1
    alt = np.where(np.arange(128) % 2 == 0, 1.0, -1.0)
    expand = np.zeros((32, 1024), np.float32)
    for r in range(4):
        for e in range(4):
            col = ((r % 2) * 4 + e) * 128
            expand[r * 8 + e, col : col + 128] = 1.0 if r < 2 else alt
    lane_sum = np.zeros((8, 256), np.float32)
    lane_sum[0] = 1
    lane_sum[1] = np.concatenate([alt, alt])
    eye = np.eye(128, dtype=np.float32)
    place = np.zeros((640, 2, 4, 2, 128), np.float32)
    for yy in range(SIDE):
        for xx in range(SIDE):
            for i in range(20):
                for ab in range(2):
                    slot = 2 * (yy * 80 + xx * 20 + i) + ab
                    place[slot, 0, xx, ab, yy * 20 + i] = 1
                    place[slot, 1, yy, ab, xx * 20 + i] = 1
    place = place.reshape(640, 2048)
    column = np.zeros((16, 1024), np.float32)
    for i in range(8):
        column[i, i * 128 : i * 128 + 128] = 64
        column[8 + i, i * 128 : i * 128 + 128] = 1
    return [
        np.asarray(t, jnp.bfloat16)
        for t in (place, eye, column, flip, spread, spread.T.copy(), expand, lane_sum)
    ]


def dft_tables():
    p = np.arange(40)
    q = np.arange(64)
    u = np.arange(64)
    v = np.arange(128)
    synth, turn_a, turn_b, back_re, back_im, gather = [], [], [], [], [], []
    for h in range(2):
        coarse = 2 * np.pi * ((p[:, None] * (2 * v[None, :] + h)) % 256) / 256
        c, s = np.cos(coarse), np.sin(coarse)
        top = np.concatenate([c.T, -s.T], 1)
        low = np.concatenate([s.T, c.T], 1)
        synth.append(np.concatenate([top, low], 0))
        turn = 2 * np.pi * ((q[None, :] * (2 * v[:, None] + h)) % 16384) / 16384
        tc, ts = np.cos(turn), np.sin(turn)
        turn_a.append(np.concatenate([tc, ts], 1))
        turn_b.append(np.concatenate([-ts, tc], 1))
        back_re.append(tc.T.copy())
        back_im.append(ts.T.copy())
        gather.append(
            np.concatenate([np.concatenate([c, s], 1), np.concatenate([-s, c], 1)], 0)
        )
    fine = 2 * np.pi * ((q[None, :] * u[:, None]) % 64) / 64
    fc, fs = np.cos(fine), np.sin(fine)
    fine_out = np.concatenate([fc, -fs], 1)
    fine_in = np.concatenate([fc.T, -fs.T], 0)
    weight = np.full((80, 128), 2.0)
    weight[0, 0] = weight[40, 0] = weight[0, 64] = weight[40, 64] = 1.0

    def split(t):
        t = np.asarray(t, np.float32)
        hi = t.astype(jnp.bfloat16)
        lo = (t - hi.astype(np.float32)).astype(jnp.bfloat16)
        return np.concatenate([hi, lo, hi], axis=-1)

    return [
        split(np.stack(synth)),
        np.stack(turn_a).astype(np.float32),
        np.stack(turn_b).astype(np.float32),
        np.stack(back_re).astype(np.float32),
        np.stack(back_im).astype(np.float32),
        split(np.stack(gather)),
        split(fine_out),
        split(fine_in),
        weight.astype(np.float32),
    ]


OPERANDS = (
    "order", "place", "eye", "column", "noise", "amp", "flip", "spread", "spread_t", "expand",
    "lane_sum", "synth", "turn_a", "turn_b", "back_re", "back_im", "gather", "fine_out", "fine_in", "weight",
    "cnt", "msk",
)


def kernel(leg, *refs):
    count = len(OPERANDS)
    sources, out, local = refs[:count], refs[count], refs[count + 1 : 2 * count + 1]
    (
        op_sem,
        lg, wide, ls_x, ls_y, lr_x, lr_y, hg1_x, hg1_y, hg_x, hg_y, hst, accs, fsend, frecv, pt, qt,
        bsend, brecv, psend, precv, coef, gst_x, gst_y, gs1_x, gs1_y, gr1_x, gr1_y, gs2_x, gs2_y, gr2_x, gr2_y,
        digs, dig, thr, own_thr, rows16, h_even, h_odd, hpack, harm_x, harm_y, tot, full_acc,
        lg_sem, ls_sem, lrecv_sem, h1s, h1r, h2s, h2r, fs_sem, fr_sem, bs_sem, br_sem,
        ps_sem, pr_sem, g1s, g1r, g2s, g2r,
    ) = refs[2 * count + 1 :]
    hg1, hg, harm = (hg1_x, hg1_y), (hg_x, hg_y), (harm_x, harm_y)
    gst, gs1, gr1, gs2, gr2 = (gst_x, gst_y), (gs1_x, gs1_y), (gr1_x, gr1_y), (gs2_x, gs2_y), (gr2_x, gr2_y)
    fetches = [
        pltpu.make_async_copy(sources[i], local[i], op_sem.at[i]) for i in range(count)
    ]
    for i in range(7):
        fetches[i].start()
    arrived = set()

    def need(*names):
        for name in names:
            i = OPERANDS.index(name)
            if i not in arrived:
                arrived.add(i)
                fetches[i].wait()

    (
        order, place_, eye, column, noise, amp, flip, spread, spread_t, expand,
        lane_sum, synth, turn_a, turn_b, back_re, back_im, gather, fine_out, fine_in, weight,
        cnt, msk,
    ) = local
    b = lax.axis_index("blk")
    g = lax.axis_index("ma")
    y, x, z = b // 16, (b // 4) % 4, b % 4
    pending = []

    def at(yy, xx, zz, gg):
        return (yy * 16 + xx * 4 + zz, gg)

    def shift(v, d):
        return lax.rem(v + d, 4) if d else v

    def remote(src, dst, ssem, rsem, dev):
        return pltpu.make_async_remote_copy(
            src_ref=src, dst_ref=dst, send_sem=ssem, recv_sem=rsem, device_id=dev, device_id_type=MESH
        )

    def send(src, dst, ssem, rsem, dev):
        c = remote(src, dst, ssem, rsem, dev)
        c.start()
        pending.append(c)

    peers = []
    for dx in range(4):
        for dg in range(4):
            if dx or dg:
                peers.append((0, dx, 0, dg))
    for dy in range(1, 4):
        for dg in range(4):
            peers.append((dy, 0, 0, dg))
    for dy in range(4):
        for dz in range(1, 4):
            peers.append((dy, 0, dz, 0))
    barrier = pltpu.get_barrier_semaphore()
    for dy, dx, dz, dg in peers:
        pl.semaphore_signal(
            barrier, inc=1, device_id=at(shift(y, dy), shift(x, dx), shift(z, dz), shift(g, dg)),
            device_id_type=MESH,
        )

    steps = (1, 3, 2, 0)
    loads = {}
    for d in steps:
        yy = shift(y, d)
        rows = pl.ds(pl.multiple_of(yy * 160, 32), 160)
        for n in range(2):
            c = pltpu.make_async_copy(leg.at[n, rows], lg.at[n, rows], lg_sem.at[n, d])
            c.start()
            loads[d, n] = c

    for i in range(7, count):
        fetches[i].start()
    accs[...] = jnp.zeros_like(accs)
    dig[...] = jnp.zeros_like(dig)
    h_even[...] = jnp.zeros_like(h_even)
    h_odd[...] = jnp.zeros_like(h_odd)
    hpack[...] = jnp.zeros_like(hpack)

    def row_of(rows, i):
        at_row = lax.broadcasted_iota(jnp.int32, rows.shape, 0) == i
        return jnp.sum(jnp.where(at_row, rows, 0.0), axis=0, keepdims=True)

    need("order", "place", "eye", "column")
    slots = order[...].reshape(1, order.shape[0])
    high = (slots >> 6).astype(F32)
    low = (slots & 63).astype(F32)
    for gg in range(4):
        dig[gg : gg + 1, :] = high[:, gg * 640 : gg * 640 + 640]
        dig[8 + gg : 9 + gg, :] = low[:, gg * 640 : gg * 640 + 640]
    placed = nn(dig[...].astype(BF16), place_[...])
    for i in range(16):
        digs[i] = placed[i : i + 1]
    for i in range(8):
        rows16[i : i + 1, :] = digs[g, :, i * 256 : i * 256 + 128]
        rows16[8 + i : 9 + i, :] = digs[g + 8, :, i * 256 : i * 256 + 128]
    lane80 = lax.broadcasted_iota(jnp.int32, (80, 128), 1).astype(F32)
    across16 = nt(eye[...], rows16[...].astype(BF16))
    spreads = nn(across16[0:80].astype(BF16), column[...])
    for i in range(8):
        thr[i // 4, i % 4] = spreads[:, i * 128 : i * 128 + 128] + 128.0 - lane80

    need("noise", "amp", "flip")
    own_thr[...] = jnp.zeros_like(own_thr)
    for k in range(OWN):
        line = row_of(thr[1, y], x * 20 + z * OWN + k)
        own_thr[2 * k : 2 * k + 1, :] = line
        own_thr[2 * k + 1 : 2 * k + 2, :] = line
        h_even[2 * k : 2 * k + 2, :] = noise[2 * k]
        h_odd[2 * k : 2 * k + 2, :] = noise[2 * k + 1]
    own_limit = own_thr[...]
    scale = amp[...].reshape(1, amp.shape[0])

    def where_packed(t):
        m, o = (0, t) if t < XT else (1, t - XT)
        return m, (o // PIECE[m]) * 10, (o % PIECE[m]) * 128

    for t in range(XT + YT):
        m, r0, c0 = where_packed(t)
        value = None
        if t > 0:
            cols = slice((t - 1) * 128, t * 128)
            value = (h_even[:, cols] * scale[:, cols]).astype(BF16).astype(F32)
        if t < XT + YT - 1:
            cols = slice((19 - t) * 128, (20 - t) * 128)
            flipped = nn((h_odd[:, cols] * scale[:, cols]).astype(BF16), flip[128:256, 0:128])
        else:
            flipped = jnp.zeros((16, 128), F32)
        flipped = jnp.where(own_limit >= 128.0 * (t + 1), flipped, 0.0)
        value = flipped if value is None else jnp.where(own_limit <= 128.0 * t, value, flipped)
        hpack[m, r0 : r0 + 10, c0 : c0 + 128] = value[0:10]
    harm[0][...] = hpack[0].astype(BF16)
    harm[1][...] = hpack[1, :, 0:384].astype(BF16)

    def harmonics_copy(stage, m, d, arriving):
        axis = (z, y) if m == 0 else (x, z)
        here = axis[stage]
        there = shift(here, d)
        slot = there if arriving else here
        who = (at(y, x, there, g), at(there, x, z, g)) if m == 0 else (at(y, there, z, g), at(y, x, there, g))
        if stage == 0:
            return remote(harm[m], hg1[m].at[slot], h1s.at[m, d], h1r.at[m, slot], who[0])
        target = hg[0].at[slot] if m == 0 else hg[1].at[:, slot]
        return remote(hg1[m], target, h2s.at[m, d], h2r.at[m, slot], who[1])

    def begin(c):
        c.start()
        pending.append(c)

    def widen(yy):
        rows = pl.ds(pl.multiple_of(yy * 160, 32), 160)

        def body(i, carry):
            n, s = i // 20, i % 20
            block = lg[n, rows, pl.ds(pl.multiple_of(s * 128, 128), 128)].astype(F32)
            wide[n, s, pl.ds(yy * 4, 4)] = block.reshape(4, 40, 128)
            return carry

        lax.fori_loop(0, 40, body, 0, unroll=4)

    def pack(mode, dest):
        buf = (ls_x, ls_y)[mode]
        blocks = [k * 4 + dest if mode == 0 else dest * 4 + k for k in range(4)]
        first, last = (0, XT) if mode == 0 else (XT, XT + YT)

        def one(n, carry):
            def take(s, ab):
                parts = []
                for i in (0, 2):
                    p, q = wide.at[n, s, blocks[i]], wide.at[n, s, blocks[i + 1]]
                    parts.append(p[pl.ds(ab, 16, stride=2), :])
                    parts.append(
                        jnp.concatenate([p[pl.ds(32 + ab, 4, stride=2), :], q[pl.ds(ab, 4, stride=2), :]], axis=0)
                    )
                    parts.append(q[pl.ds(8 + ab, 16, stride=2), :])
                return jnp.concatenate(parts, axis=0)

            pairs = range(first, min(last, 20), 2)
            tall = [
                jnp.concatenate([take(18 - t, 1), take(19 - t, 1)], axis=1).astype(BF16) for t in pairs
            ]
            flipped = nn(jnp.concatenate(tall, axis=0), flip[...])
            limit = thr[mode, dest]
            for t in range(first, last):
                o = (t - first) * 128
                if t < 20:
                    r = ((t - first) // 2) * 80
                    c = ((t - first) % 2) * 128
                    back = flipped[r : r + 80, c : c + 128]
                if t == 0:
                    mix = back
                elif t == 20:
                    mix = take(19, 0)
                else:
                    mix = jnp.where(limit <= 128.0 * t, take(t - 1, 0), back)
                buf[dest, n, :, o : o + 128] = mix.astype(BF16)
            return carry

        lax.fori_loop(0, 2, one, 0)

    send_bufs, recv_bufs = (ls_x, ls_y), (lr_x, lr_y)

    def place(mode, other, r):
        return at(y, other, z, r) if mode == 0 else at(other, x, z, r)

    def mine(mode):
        return x if mode == 0 else y

    def give(mode, d, n):
        dest = shift(mine(mode), d)
        send(
            send_bufs[mode].at[dest, n], recv_bufs[mode].at[mine(mode), n],
            ls_sem.at[mode, d, n], lrecv_sem.at[mode, mine(mode), n], place(mode, dest, g),
        )

    for d in steps:
        for n in range(2):
            loads[d, n].wait()
        widen(shift(y, d))
    pack(0, shift(x, 1))

    pl.semaphore_wait(barrier, len(peers))

    for m in (1, 0):
        for d in (1, 3, 2):
            begin(harmonics_copy(0, m, d, False))
    hg1[0][z] = harm[0][...]
    hg1[1][x] = harm[1][...]
    give(0, 1, 0)
    give(0, 1, 1)
    pack(1, shift(y, 1))
    give(1, 1, 0)
    pack(0, shift(x, 3))
    give(0, 3, 0)
    give(0, 3, 1)
    pack(1, shift(y, 3))
    give(1, 3, 0)
    for m in (0, 1):
        for d in (1, 3, 2):
            harmonics_copy(0, m, d, True).wait_recv()
        for d in (1, 3, 2):
            begin(harmonics_copy(1, m, d, False))
    give(1, 1, 1)
    give(1, 3, 1)
    hg[0][y] = hg1[0][...]
    hg[1][:, z] = hg1[1][...]
    pack(0, shift(x, 2))
    give(0, 2, 0)
    give(0, 2, 1)
    pack(1, shift(y, 2))
    give(1, 2, 0)
    give(1, 2, 1)
    for mode in (1, 0):
        own = mine(mode)
        pack(mode, own)
        recv_bufs[mode][own] = send_bufs[mode][own]

    def digits(i, carry):
        col = pl.ds(pl.multiple_of((i // 4) * 256, 256), 256)
        who = i % 4
        used = (lax.broadcasted_iota(jnp.int32, (1, 256), 1) & 127) < 80
        hi = jnp.where(used, digs[who, :, col], -1.0).astype(jnp.int32)
        lo = digs[who + 8, :, col].astype(jnp.int32)
        pt[i] = jnp.where(
            lax.broadcasted_iota(jnp.int32, (40, 256), 0) == hi, 1.0, 0.0
        ).astype(F32)
        qt[i] = jnp.where(
            (lax.broadcasted_iota(jnp.int32, (128, 256), 0) & 63) == lo, 1.0, 0.0
        ).astype(BF16)
        return carry

    lax.fori_loop(0, 32, digits, 0)

    need("spread_t", "lane_sum")

    def parity(mode):
        line = row_of(rows16[...], 8 + mode * 4 + mine(mode)).astype(jnp.int32)
        return jnp.where((line & 1) == 1, -1.0, 1.0)

    full_acc[...] = jnp.zeros_like(full_acc)
    for m in range(2):
        for dd in (1, 3, 2):
            harmonics_copy(1, m, dd, True).wait_recv()
        width = PIECE[m] * 128
        blocks = hg[m][...].reshape(512, width)

        for c0 in range(0, width, 256):
            c1 = min(width, c0 + 256)
            hst[m, :, c0:c1] = nn(spread_t[...], blocks[:, c0:c1])

    def synthesize(mode, src):
        tiles = (XT, YT)[mode]
        table = recv_bufs[mode]
        own = mine(mode)

        def group(i, carry):
            r0 = pl.multiple_of(i * 16, 16)
            rows = pl.ds(r0, 16)
            limit = thr[mode, own, rows, :]
            total = [[None, None], [None, None]]
            upper = [[None, None], [None, None]]
            for t in range(tiles):
                tile = t + (0 if mode == 0 else XT)
                is_a = limit <= 128 * tile
                for c in range(2):
                    row = pl.ds(pl.multiple_of(((t // PIECE[mode]) * 2 + c) * 80 + r0, 16), 16)
                    h = hst[mode, row, (t % PIECE[mode]) * 128 : (t % PIECE[mode]) * 128 + 128]
                    for n in range(2):
                        v = table[src, n, rows, t * 128 : t * 128 + 128].astype(F32) * h
                        w = jnp.where(is_a, v, 0.0)
                        total[n][c] = v if t == 0 else total[n][c] + v
                        upper[n][c] = w if t == 0 else upper[n][c] + w
            for n in range(2):
                for c in range(2):
                    accs[n, 2 * c, rows, :] = upper[n][c]
                    accs[n, 2 * c + 1, rows, :] = total[n][c] - upper[n][c]
            return carry

        lax.fori_loop(0, 5, group, 0)
        sign = parity(mode)
        signs = jnp.concatenate([sign] * 4, axis=1)
        for n in range(2):
            rows = accs[n].reshape(512, 128)
            hi = rows.astype(BF16)
            lo = (rows - hi.astype(F32)).astype(BF16)
            both = nt(lane_sum[...], jnp.concatenate([hi, lo], axis=1))
            fsend[mode, src, n] = both[0:1]
            fsend[mode, src, n + 2] = both[1:2] * signs

    def scatter(mode, d):
        own = mine(mode)
        p = shift(own, (4 - d) % 4)
        total = full_acc[...]
        for e in range(4):
            r = shift(g, e)
            if d or e:
                remote(
                    fsend.at[mode, p, r], frecv.at[mode, p, r],
                    fs_sem.at[mode, d, e], fr_sem.at[mode, p, r], at(y, x, z, g),
                ).wait_recv()
            i = mode * 16 + p * 4 + r
            row = frecv[mode, p, r]
            digit = pt[i]
            both = jnp.concatenate([digit * row[:, 0:256], digit * row[:, 256:512]], axis=0)
            hi = both.astype(BF16)
            lo = (both - hi.astype(F32)).astype(BF16)
            total = total + nt(jnp.concatenate([hi, lo], axis=0), qt[i])
        full_acc[...] = total

    behind = []
    for d in (0, 3, 1, 2):
        for mode in (1, 0):
            own = mine(mode)
            src = shift(own, d)
            if d:
                for n in range(2):
                    remote(
                        send_bufs[mode].at[src, n], recv_bufs[mode].at[src, n],
                        ls_sem.at[mode, d, n], lrecv_sem.at[mode, src, n], at(y, x, z, g),
                    ).wait_recv()
            synthesize(mode, src)
            for e in range(4):
                r = shift(g, e)
                if d or e:
                    send(
                        fsend.at[mode, src, r], frecv.at[mode, own, g],
                        fs_sem.at[mode, d, e], fr_sem.at[mode, own, g], place(mode, src, r),
                    )
                else:
                    frecv[mode, own, g] = fsend[mode, src, r]
            behind.append((mode, d))
            if len(behind) > 4:
                scatter(*behind.pop(0))
    for mode, d in behind:
        scatter(mode, d)

    need(*OPERANDS)
    h = g % 2

    def halves(v):
        hi = v.astype(BF16)
        return hi, (v - hi.astype(F32)).astype(BF16)

    def thrice(v, axis):
        hi, lo = halves(v)
        return jnp.concatenate([hi, hi, lo], axis=axis)

    full = full_acc[...]
    full = (full[0:80] + full[80:160]) * weight[...]
    section = nn(synth[h], thrice(full, 0))
    turned = section[0:128] * turn_a[h] + section[128:256] * turn_b[h]
    log_density = nt(fine_out[...], thrice(turned, 1))
    inside = msk[...].astype(F32)
    number = inside * cnt[...].astype(F32)
    dens = inside * jnp.exp(log_density)
    psend[0, 0] = jnp.concatenate(
        [jnp.sum(dens, axis=0, keepdims=True), jnp.sum(number, axis=0, keepdims=True)], axis=1
    )
    precv[0, x, g] = psend[0, 0]
    for d in range(4):
        for e in range(4):
            if d or e:
                send(
                    psend.at[0, 0], precv.at[0, x, g], ps_sem.at[0, d, e], pr_sem.at[0, x, g],
                    at(y, shift(x, d), z, shift(g, e)),
                )

    first = nn(fine_in[...], thrice(jnp.concatenate([number, dens], axis=1), 0))
    lines = []
    for f in range(2):
        re, im = first[0:64, f * 128 : f * 128 + 128], first[64:128, f * 128 : f * 128 + 128]
        tre = re * back_re[h] + im * back_im[h]
        tim = im * back_re[h] - re * back_im[h]
        line = thrice(jnp.concatenate([tre, tim], axis=1), 1)
        lines += [line, line]
    modes = nt(gather[h], jnp.concatenate(lines, axis=0))
    modes = jnp.concatenate([modes[:, 0:128] * weight[...], modes[:, 128:256] * weight[...]], axis=0)
    modes_hi = modes.astype(BF16).astype(F32)
    lane = lax.broadcasted_iota(jnp.int32, (160, 128), 1)
    modes = jnp.where(lane < 64, modes_hi, modes - modes_hi).astype(BF16)

    def second_sums():
        for d in range(4):
            for e in range(4):
                if d or e:
                    xx, gg = shift(x, d), shift(g, e)
                    remote(
                        psend.at[0, 0], precv.at[0, xx, gg], ps_sem.at[0, d, e], pr_sem.at[0, xx, gg],
                        at(y, x, z, g),
                    ).wait_recv()
        psend[1, 0] = jnp.sum(precv[0].reshape(16, 1, 256), axis=0)
        precv[1, y, z] = psend[1, 0]
        for d in range(4):
            for e in range(4):
                if d or e:
                    send(
                        psend.at[1, 0], precv.at[1, y, z], ps_sem.at[1, d, e], pr_sem.at[1, y, z],
                        at(shift(y, d), x, shift(z, e), g),
                    )

    for mode in (0, 1):
        own = mine(mode)
        if mode == 1:
            second_sums()
        for d in (2, 1, 3, 0):
            p = shift(own, d)
            for e in range(4):
                gg = shift(g, e)
                i = mode * 16 + p * 4 + gg
                rows = nn(modes, qt[i])
                digit = pt[i]
                for k in range(4):
                    line = jnp.sum(rows[k * 40 : k * 40 + 40] * digit, axis=0, keepdims=True)
                    for ab in range(2):
                        bsend[mode, p, gg, 2 * k + ab : 2 * k + ab + 1, :] = line[:, ab * 128 : ab * 128 + 128]
                if d or e:
                    send(
                        bsend.at[mode, p, gg], brecv.at[mode, own, g],
                        bs_sem.at[mode, d, e], br_sem.at[mode, own, g], place(mode, p, gg),
                    )
                else:
                    brecv[mode, own, g] = bsend[mode, p, gg]

    for d in range(4):
        for e in range(4):
            if d or e:
                yy, zz = shift(y, d), shift(z, e)
                remote(
                    psend.at[1, 0], precv.at[1, yy, zz], ps_sem.at[1, d, e], pr_sem.at[1, yy, zz],
                    at(y, x, z, g),
                ).wait_recv()
    sums = jnp.sum(precv[1].reshape(16, 1, 256), axis=0)
    ratio = jnp.sum(sums[:, 128:256], axis=1, keepdims=True) / jnp.sum(
        sums[:, 0:128], axis=1, keepdims=True
    )

    def analyse(mode):
        tiles = (XT, YT)[mode]
        own = mine(mode)
        for d in range(4):
            for e in range(4):
                if d or e:
                    p, r = shift(own, d), shift(g, e)
                    remote(
                        bsend.at[mode, p, r], brecv.at[mode, p, r],
                        bs_sem.at[mode, d, e], br_sem.at[mode, p, r], at(y, x, z, g),
                    ).wait_recv()
        sign = parity(mode)
        for p in range(4):
            lines = []
            for r in range(4):
                tile = brecv[mode, p, r]
                line = tile - ratio * pltpu.roll(tile, 4, 0)
                line = jnp.where(lax.broadcasted_iota(jnp.int32, (8, 128), 0) < 4, line, 0.0)
                lines.append(line if r < 2 else line * sign)
            across = nt(eye[...], jnp.concatenate(lines, axis=0).astype(BF16))
            coef[p] = nn(across[0:80].astype(BF16), expand[...])
        table = recv_bufs[mode]

        def group(i, carry):
            r0 = pl.multiple_of(i * 16, 16)
            rows = pl.ds(r0, 16)
            limit = thr[mode, own, rows, :]
            for c in range(2):
                co = [
                    [
                        [coef[p, rows, ((n * 2 + c) * 2 + ab) * 128 : ((n * 2 + c) * 2 + ab) * 128 + 128] for ab in range(2)]
                        for n in range(2)
                    ]
                    for p in range(4)
                ]
                for t in range(tiles):
                    is_a = limit <= 128 * (t + (0 if mode == 0 else XT))
                    total = None
                    for p in range(4):
                        for n in range(2):
                            v = table[p, n, rows, t * 128 : t * 128 + 128].astype(F32) * jnp.where(
                                is_a, co[p][n][0], co[p][n][1]
                            )
                            total = v if total is None else total + v
                    row = pl.ds(pl.multiple_of(((t // PIECE[mode]) * 2 + c) * 80 + r0, 16), 16)
                    gst[mode][row, (t % PIECE[mode]) * 128 : (t % PIECE[mode]) * 128 + 128] = total.astype(BF16)
            return carry

        lax.fori_loop(0, 5, group, 0)
        across = y if mode == 0 else x
        for d in (1, 3, 2, 0):
            dest = shift(across, d)
            rows = pl.ds(pl.multiple_of(dest * 128, 128), 128)
            part = nn(spread[rows, :], gst[mode][...]).astype(BF16)
            if d:
                gs1[mode][dest] = part
                who = at(dest, x, z, g) if mode == 0 else at(y, dest, z, g)
                send(
                    gs1[mode].at[dest], gr1[mode].at[across], g1s.at[mode, d], g1r.at[mode, across], who
                )
            else:
                gr1[mode][across] = part

    for mode in (0, 1):
        analyse(mode)

    def sum4(ref):
        total = ref[0].astype(F32)
        for k in range(1, 4):
            total = total + ref[k].astype(F32)
        return total

    for mode in (0, 1):
        across = y if mode == 0 else x
        for d in (1, 3, 2):
            src = shift(across, d)
            remote(
                gs1[mode].at[src], gr1[mode].at[src], g1s.at[mode, d], g1r.at[mode, src], at(y, x, z, g)
            ).wait_recv()
        gs2[mode][...] = sum4(gr1[mode]).astype(BF16).reshape(4, 32, PIECE[mode] * 128)
        gr2[mode][z] = gs2[mode][z]
        for d in (1, 3, 2):
            dest = shift(z, d)
            send(
                gs2[mode].at[dest], gr2[mode].at[z], g2s.at[mode, d], g2r.at[mode, z], at(y, x, dest, g)
            )
    for mode in (1, 0):
        for d in (1, 3, 2):
            src = shift(z, d)
            remote(
                gs2[mode].at[src], gr2[mode].at[src], g2s.at[mode, d], g2r.at[mode, src], at(y, x, z, g)
            ).wait_recv()
        tot[mode, :, 0 : PIECE[mode] * 128] = sum4(gr2[mode])

    own_order = own_limit - 128.0 + lax.broadcasted_iota(jnp.int32, (16, 128), 1).astype(F32)
    lane10 = lax.broadcasted_iota(jnp.int32, (10, 128), 1).astype(F32)
    for t in range(XT + YT):
        m, r0, c0 = where_packed(t)
        value = tot[m, r0 : r0 + 10, c0 : c0 + 128]
        if t > 0:
            cols = slice((t - 1) * 128, t * 128)
            even = jnp.where(own_limit[0:10] <= 128.0 * t, value, 0.0)
            for k in range(OWN):
                out[2 * k, :, cols] = even[2 * k : 2 * k + 2]
        if t < XT + YT - 1:
            s = 19 - t
            cols = slice(s * 128, s * 128 + 128)
            hi = value.astype(BF16)
            lo = (value - hi.astype(F32)).astype(BF16)
            back = nn(hi, flip[128:256, 0:128]) + nn(lo, flip[128:256, 0:128])
            odd = jnp.where(own_order[0:10] + lane10 >= 2559.0 - 128.0 * s, back, 0.0)
            for k in range(OWN):
                out[2 * k + 1, :, cols] = odd[2 * k : 2 * k + 2]

    for c in pending:
        c.wait_send()


def per_device(white_noise, amplitude, legendre, order_of_slot, counts, survey_mask):
    tables = [jnp.asarray(t) for t in selection_tables()]
    operands = (
        [order_of_slot] + tables[:3] + [white_noise, amplitude] + tables[3:]
        + [jnp.asarray(t) for t in dft_tables()]
        + [counts.reshape(64, 128), survey_mask.reshape(64, 128)]
    )
    vmem = pl.BlockSpec(memory_space=pltpu.VMEM)
    dma = pltpu.SemaphoreType.DMA
    got = pl.pallas_call(
        kernel,
        out_shape=jax.ShapeDtypeStruct(white_noise.shape, F32),
        in_specs=[pl.BlockSpec(memory_space=pl.ANY)] * (1 + len(operands)),
        out_specs=vmem,
        scratch_shapes=[pltpu.VMEM(o.shape, o.dtype) for o in operands]
        + [
            dma((len(operands),)),
            pltpu.VMEM((2, 640, 2560), BF16),
            pltpu.VMEM((2, 20, 16, 40, 128), F32),
            pltpu.VMEM((4, 2, 80, LANES[0]), BF16),
            pltpu.VMEM((4, 2, 80, LANES[1]), BF16),
            pltpu.VMEM((4, 2, 80, LANES[0]), BF16),
            pltpu.VMEM((4, 2, 80, LANES[1]), BF16),
            pltpu.VMEM((4, 32, 512), BF16),
            pltpu.VMEM((4, 32, 384), BF16),
            pltpu.VMEM((4, 4, 32, 512), BF16),
            pltpu.VMEM((4, 4, 32, 384), BF16),
            pltpu.VMEM((2, 480, 512), F32),
            pltpu.VMEM((2, 4, 128, 128), F32),
            pltpu.VMEM((2, 4, 4, 1, 512), F32),
            pltpu.VMEM((2, 4, 4, 1, 512), F32),
            pltpu.VMEM((32, 40, 256), F32),
            pltpu.VMEM((32, 128, 256), BF16),
            pltpu.VMEM((2, 4, 4, 8, 128), F32),
            pltpu.VMEM((2, 4, 4, 8, 128), F32),
            pltpu.VMEM((2, 1, 1, 256), F32),
            pltpu.VMEM((2, 4, 4, 1, 256), F32),
            pltpu.VMEM((4, 80, 1024), F32),
            pltpu.VMEM((480, 512), BF16),
            pltpu.VMEM((480, 384), BF16),
            pltpu.VMEM((4, 128, 512), BF16),
            pltpu.VMEM((4, 128, 384), BF16),
            pltpu.VMEM((4, 128, 512), BF16),
            pltpu.VMEM((4, 128, 384), BF16),
            pltpu.VMEM((4, 32, 512), BF16),
            pltpu.VMEM((4, 32, 384), BF16),
            pltpu.VMEM((4, 32, 512), BF16),
            pltpu.VMEM((4, 32, 384), BF16),
            pltpu.VMEM((16, 1, 2048), F32),
            pltpu.VMEM((16, 640), F32),
            pltpu.VMEM((2, 4, 80, 128), F32),
            pltpu.VMEM((16, 128), F32),
            pltpu.VMEM((16, 128), F32),
            pltpu.VMEM((16, 2560), F32),
            pltpu.VMEM((16, 2560), F32),
            pltpu.VMEM((2, 32, 512), F32),
            pltpu.VMEM((32, 512), BF16),
            pltpu.VMEM((32, 384), BF16),
            pltpu.VMEM((2, 32, 512), F32),
            pltpu.VMEM((160, 128), F32),
            dma((2, 4)),
            dma((2, 4, 2)),
            dma((2, 4, 2)),
            dma((2, 4)),
            dma((2, 4)),
            dma((2, 4)),
            dma((2, 4)),
            dma((2, 4, 4)),
            dma((2, 4, 4)),
            dma((2, 4, 4)),
            dma((2, 4, 4)),
            dma((2, 4, 4)),
            dma((2, 4, 4)),
            dma((2, 4)),
            dma((2, 4)),
            dma((2, 4)),
            dma((2, 4)),
        ],
        compiler_params=pltpu.CompilerParams(
            collective_id=0, has_side_effects=True, vmem_limit_bytes=58 * 1024 * 1024
        ),
        name="survey",
    )(legendre, *operands)
    return got * amplitude


def solution(mesh):
    placed = (
        P(("ma", "blk"), None, None),
        P(),
        P("blk", "ma", None),
        P(),
        P(("blk", "ma"), None),
        P(("blk", "ma"), None),
    )
    return jax.shard_map(
        per_device,
        mesh=mesh,
        in_specs=placed,
        out_specs=P(("ma", "blk"), None, None),
        check_vma=False,
    )
```

time: 120 us -> 79.4 us (0.66)
  local copies, waits for them, and re-layouts: 23.7 us -> 0.01 us
  Pallas kernels: 91.8 us -> 77.1 us
  other arithmetic: 3.16 us -> 1.69 us
    unnamed x41 -> x2, local copies, waits for them, and re-layouts: 16.3 us -> 0.01 us
    pallas_call x1, Pallas kernels: 91.8 us -> 77.1 us  [per_device(): pl.pallas_call(kernel, out_shape=jax.ShapeDtypeStruct(white_noise.shape,...]
    rev x2 -> x0, local copies, waits for them, and re-layouts: 3.87 us -> none  [the longest x1 1.96 us: per_device(): pairs[:, 1, :, ::-1]]
    mul x0 -> x1, other arithmetic: none -> 1.69 us  [per_device(): return got * amplitude]
where the time goes in v2:
time: 79.4 us; the launch traced here: 78.9 us
  Pallas kernels  77.1 us (97%)
  other arithmetic  1.69 us (2%)
    pallas_call x1, Pallas kernels, per_device(): pl.pallas_call(kernel, out_shape=jax.ShapeDtypeStruct(white_noise.shape,...  77.1 us
    mul x1, other arithmetic, per_device(): return got * amplitude  1.69 us

profile of v2, /device:TPU:2, one launch (start us, length us, event | category | flops | bytes accessed | tf_op | source)
XLA Modules:
  0.0 78.9 jit_solution(7185699858692613929)
XLA Ops:
  0.0 0.0 copy-start
  0.0 77.1 %survey.1 = f32[10,2,2560]{2,1,0:T(2,128)} custom-call(bf16[2,640,2560]{2,1,0:T(8,128)(2,1)} %leg.1, s32[2560]{0:T(1024)} %refs_0_.1, bf16[640,2048]{1,0:T(8,128)(2,1)} %constant.34.clone.refs_1_, bf16[128,128]{1,0:T(8,128)(2,1)} %constant.35.clone.refs_2_, bf16[16,1024]{1,0:T(8,128)(2,1)} %constant.36.clone.refs_3_, f32[10,2,2560]{2,1,0:T(2,128)} %refs_4_.1, ...), custom_call_target="tpu_custom_call" | custom-call | tf_op jit(solution)/shard_map/survey/pallas_call | solution.py:739
  77.2 0.0 copy-done
  77.2 1.7 %broadcast_multiply_fusion = f32[10,2,2560]{2,1,0:T(2,128)} fusion(f32[10,2,2560]{2,1,0:T(2,128)} %survey.1, f32[2560]{0:T(1024)S(1)} %copy-done), kind=kLoop, calls=%fused_computation | loop fusion | flops 51200 | bytes 419840 | tf_op jit(solution)/shard_map/mul | solution.py:813
Async XLA Ops:
  0.0 77.2 %copy-start = (f32[2560]{0:T(1024)S(1)}, f32[2560]{0:T(1024)}, u32[]{:S(2)}) copy-start(f32[2560]{0:T(1024)} %refs_5_.1) | copy-start | bytes 30724

commit v3 on v2

--- a/solution.py
+++ b/solution.py
@@ -34,12 +34,11 @@
 
 def selection_tables():
     flip = np.fliplr(np.eye(256, dtype=np.float32))
-    spread = np.zeros((512, 480), np.float32)
+    spread = np.zeros((256, 240), np.float32)
     for dev in range(16):
         for j in range(3):
-            for c in range(2):
-                for k in range(OWN):
-                    spread[dev * 32 + j * 10 + 2 * k + c, (j * 2 + c) * 80 + dev * OWN + k] = 1
+            for k in range(OWN):
+                spread[dev * 16 + j * OWN + k, j * 80 + dev * OWN + k] = 1
     alt = np.where(np.arange(128) % 2 == 0, 1.0, -1.0)
     expand = np.zeros((32, 1024), np.float32)
     for r in range(4):
@@ -187,6 +186,7 @@
     for dy in range(4):
         for dz in range(1, 4):
             peers.append((dy, 0, dz, 0))
+    peers = [q for q in peers if sum(1 for v in q if v) == 1]
     barrier = pltpu.get_barrier_semaphore()
     for dy, dx, dz, dg in peers:
         pl.semaphore_signal(
@@ -197,12 +197,15 @@
     steps = (1, 3, 2, 0)
     loads = {}
     for d in steps:
-        yy = shift(y, d)
-        rows = pl.ds(pl.multiple_of(yy * 160, 32), 160)
+        xx = shift(x, d)
         for n in range(2):
-            c = pltpu.make_async_copy(leg.at[n, rows], lg.at[n, rows], lg_sem.at[n, d])
-            c.start()
-            loads[d, n] = c
+            for yy in range(4):
+                start = pl.multiple_of(yy * 160 + (xx // 2) * 80 + (xx % 2) * 32, 16)
+                c = pltpu.make_async_copy(
+                    leg.at[n, pl.ds(start, 48)], lg.at[n, yy, xx], lg_sem.at[d, n, yy]
+                )
+                c.start()
+                loads[d, n, yy] = c
 
     for i in range(7, count):
         fetches[i].start()
@@ -239,16 +242,16 @@
     own_thr[...] = jnp.zeros_like(own_thr)
     for k in range(OWN):
         line = row_of(thr[1, y], x * 20 + z * OWN + k)
-        own_thr[2 * k : 2 * k + 1, :] = line
-        own_thr[2 * k + 1 : 2 * k + 2, :] = line
-        h_even[2 * k : 2 * k + 2, :] = noise[2 * k]
-        h_odd[2 * k : 2 * k + 2, :] = noise[2 * k + 1]
+        for c in range(2):
+            own_thr[8 * c + k : 8 * c + k + 1, :] = line
+            h_even[8 * c + k : 8 * c + k + 1, :] = noise[2 * k, c : c + 1, :]
+            h_odd[8 * c + k : 8 * c + k + 1, :] = noise[2 * k + 1, c : c + 1, :]
     own_limit = own_thr[...]
     scale = amp[...].reshape(1, amp.shape[0])
 
     def where_packed(t):
         m, o = (0, t) if t < XT else (1, t - XT)
-        return m, (o // PIECE[m]) * 10, (o % PIECE[m]) * 128
+        return m, (o // PIECE[m]) * OWN, (o % PIECE[m]) * 128
 
     for t in range(XT + YT):
         m, r0, c0 = where_packed(t)
@@ -263,7 +266,8 @@
             flipped = jnp.zeros((16, 128), F32)
         flipped = jnp.where(own_limit >= 128.0 * (t + 1), flipped, 0.0)
         value = flipped if value is None else jnp.where(own_limit <= 128.0 * t, value, flipped)
-        hpack[m, r0 : r0 + 10, c0 : c0 + 128] = value[0:10]
+        for c in range(2):
+            hpack[m, c * 16 + r0 : c * 16 + r0 + OWN, c0 : c0 + 128] = value[8 * c : 8 * c + OWN]
     harm[0][...] = hpack[0].astype(BF16)
     harm[1][...] = hpack[1, :, 0:384].astype(BF16)
 
@@ -282,16 +286,21 @@
         c.start()
         pending.append(c)
 
-    def widen(yy):
-        rows = pl.ds(pl.multiple_of(yy * 160, 32), 160)
+    def widen(d):
+        for n in range(2):
+            for yy in range(4):
+                loads[d, n, yy].wait()
+        xx = shift(x, d)
+        top = pl.multiple_of(8 - (xx % 2) * 8, 8)
 
         def body(i, carry):
             n, s = i // 20, i % 20
-            block = lg[n, rows, pl.ds(pl.multiple_of(s * 128, 128), 128)].astype(F32)
-            wide[n, s, pl.ds(yy * 4, 4)] = block.reshape(4, 40, 128)
+            for yy in range(4):
+                block = lg[n, yy, xx, :, pl.ds(pl.multiple_of(s * 128, 128), 128)]
+                wide[n, s, yy * 4 + xx, pl.ds(top, 48), :] = block.astype(F32)
             return carry
 
-        lax.fori_loop(0, 40, body, 0, unroll=4)
+        lax.fori_loop(0, 40, body, 0, unroll=2)
 
     def pack(mode, dest):
         buf = (ls_x, ls_y)[mode]
@@ -303,11 +312,11 @@
                 parts = []
                 for i in (0, 2):
                     p, q = wide.at[n, s, blocks[i]], wide.at[n, s, blocks[i + 1]]
-                    parts.append(p[pl.ds(ab, 16, stride=2), :])
+                    parts.append(p[pl.ds(8 + ab, 16, stride=2), :])
                     parts.append(
-                        jnp.concatenate([p[pl.ds(32 + ab, 4, stride=2), :], q[pl.ds(ab, 4, stride=2), :]], axis=0)
+                        jnp.concatenate([p[pl.ds(40 + ab, 4, stride=2), :], q[pl.ds(8 + ab, 4, stride=2), :]], axis=0)
                     )
-                    parts.append(q[pl.ds(8 + ab, 16, stride=2), :])
+                    parts.append(q[pl.ds(16 + ab, 16, stride=2), :])
                 return jnp.concatenate(parts, axis=0)
 
             pairs = range(first, min(last, 20), 2)
@@ -348,10 +357,7 @@
             ls_sem.at[mode, d, n], lrecv_sem.at[mode, mine(mode), n], place(mode, dest, g),
         )
 
-    for d in steps:
-        for n in range(2):
-            loads[d, n].wait()
-        widen(shift(y, d))
+    widen(1)
     pack(0, shift(x, 1))
 
     pl.semaphore_wait(barrier, len(peers))
@@ -363,11 +369,14 @@
     hg1[1][x] = harm[1][...]
     give(0, 1, 0)
     give(0, 1, 1)
-    pack(1, shift(y, 1))
-    give(1, 1, 0)
+    widen(3)
     pack(0, shift(x, 3))
     give(0, 3, 0)
     give(0, 3, 1)
+    widen(2)
+    widen(0)
+    pack(1, shift(y, 1))
+    give(1, 1, 0)
     pack(1, shift(y, 3))
     give(1, 3, 0)
     for m in (0, 1):
@@ -417,11 +426,11 @@
         for dd in (1, 3, 2):
             harmonics_copy(1, m, dd, True).wait_recv()
         width = PIECE[m] * 128
-        blocks = hg[m][...].reshape(512, width)
-
-        for c0 in range(0, width, 256):
-            c1 = min(width, c0 + 256)
-            hst[m, :, c0:c1] = nn(spread_t[...], blocks[:, c0:c1])
+        for c in range(2):
+            blocks = hg[m][:, :, c * 16 : c * 16 + 16, :].reshape(256, width)
+            for c0 in range(0, width, 256):
+                c1 = min(width, c0 + 256)
+                hst[m, c * 240 : c * 240 + 240, c0:c1] = nn(spread_t[...], blocks[:, c0:c1])
 
     def synthesize(mode, src):
         tiles = (XT, YT)[mode]
@@ -438,7 +447,7 @@
                 tile = t + (0 if mode == 0 else XT)
                 is_a = limit <= 128 * tile
                 for c in range(2):
-                    row = pl.ds(pl.multiple_of(((t // PIECE[mode]) * 2 + c) * 80 + r0, 16), 16)
+                    row = pl.ds(pl.multiple_of((c * 3 + t // PIECE[mode]) * 80 + r0, 16), 16)
                     h = hst[mode, row, (t % PIECE[mode]) * 128 : (t % PIECE[mode]) * 128 + 128]
                     for n in range(2):
                         v = table[src, n, rows, t * 128 : t * 128 + 128].astype(F32) * h
@@ -609,8 +618,7 @@
         sums[:, 0:128], axis=1, keepdims=True
     )
 
-    def analyse(mode):
-        tiles = (XT, YT)[mode]
+    def coefficients(mode):
         own = mine(mode)
         for d in range(4):
             for e in range(4):
@@ -629,99 +637,117 @@
                 line = jnp.where(lax.broadcasted_iota(jnp.int32, (8, 128), 0) < 4, line, 0.0)
                 lines.append(line if r < 2 else line * sign)
             across = nt(eye[...], jnp.concatenate(lines, axis=0).astype(BF16))
-            coef[p] = nn(across[0:80].astype(BF16), expand[...])
+            coef[mode, p] = nn(across[0:80].astype(BF16), expand[...])
+
+    def analyse(mode, c):
+        tiles = (XT, YT)[mode]
+        own = mine(mode)
         table = recv_bufs[mode]
 
         def group(i, carry):
             r0 = pl.multiple_of(i * 16, 16)
             rows = pl.ds(r0, 16)
             limit = thr[mode, own, rows, :]
-            for c in range(2):
-                co = [
-                    [
-                        [coef[p, rows, ((n * 2 + c) * 2 + ab) * 128 : ((n * 2 + c) * 2 + ab) * 128 + 128] for ab in range(2)]
-                        for n in range(2)
-                    ]
-                    for p in range(4)
-                ]
-                for t in range(tiles):
-                    is_a = limit <= 128 * (t + (0 if mode == 0 else XT))
-                    total = None
-                    for p in range(4):
-                        for n in range(2):
-                            v = table[p, n, rows, t * 128 : t * 128 + 128].astype(F32) * jnp.where(
-                                is_a, co[p][n][0], co[p][n][1]
-                            )
-                            total = v if total is None else total + v
-                    row = pl.ds(pl.multiple_of(((t // PIECE[mode]) * 2 + c) * 80 + r0, 16), 16)
-                    gst[mode][row, (t % PIECE[mode]) * 128 : (t % PIECE[mode]) * 128 + 128] = total.astype(BF16)
+            co = []
+            for p in range(4):
+                for n in range(2):
+                    at_lane = ((n * 2 + c) * 2) * 128
+                    co.append(
+                        (
+                            coef[mode, p, rows, at_lane : at_lane + 128],
+                            coef[mode, p, rows, at_lane + 128 : at_lane + 256],
+                        )
+                    )
+            for t in range(tiles):
+                is_a = limit <= 128.0 * (t + (0 if mode == 0 else XT))
+                total = None
+                for p in range(4):
+                    for n in range(2):
+                        v = table[p, n, rows, t * 128 : t * 128 + 128].astype(F32) * jnp.where(
+                            is_a, co[2 * p + n][0], co[2 * p + n][1]
+                        )
+                        total = v if total is None else total + v
+                row = pl.ds(pl.multiple_of((c * 3 + t // PIECE[mode]) * 80 + r0, 16), 16)
+                at_lane = (t % PIECE[mode]) * 128
+                gst[mode][row, at_lane : at_lane + 128] = total.astype(BF16)
             return carry
 
         lax.fori_loop(0, 5, group, 0)
         across = y if mode == 0 else x
         for d in (1, 3, 2, 0):
             dest = shift(across, d)
-            rows = pl.ds(pl.multiple_of(dest * 128, 128), 128)
-            part = nn(spread[rows, :], gst[mode][...]).astype(BF16)
+            rows = pl.ds(pl.multiple_of(dest * 64, 64), 64)
+            part = nn(spread[rows, :], gst[mode][c * 240 : c * 240 + 240, :]).astype(BF16)
             if d:
-                gs1[mode][dest] = part
-                who = at(dest, x, z, g) if mode == 0 else at(y, dest, z, g)
-                send(
-                    gs1[mode].at[dest], gr1[mode].at[across], g1s.at[mode, d], g1r.at[mode, across], who
-                )
+                gs1[mode][c, dest] = part
+                begin(first_sum(mode, c, d, False))
             else:
-                gr1[mode][across] = part
-
-    for mode in (0, 1):
-        analyse(mode)
-
-    def sum4(ref):
-        total = ref[0].astype(F32)
+                gr1[mode][c, across] = part
+
+    def first_sum(mode, c, d, arriving):
+        across = y if mode == 0 else x
+        there = shift(across, d)
+        slot = there if arriving else across
+        who = at(there, x, z, g) if mode == 0 else at(y, there, z, g)
+        return remote(
+            gs1[mode].at[c, there], gr1[mode].at[c, slot], g1s.at[mode, c, d], g1r.at[mode, c, slot], who
+        )
+
+    def second_sum(mode, c, d, arriving):
+        there = shift(z, d)
+        slot = there if arriving else z
+        return remote(
+            gs2[mode].at[c, there], gr2[mode].at[c, slot], g2s.at[mode, c, d], g2r.at[mode, c, slot],
+            at(y, x, there, g),
+        )
+
+    def sum4(ref, c):
+        total = ref[c, 0].astype(F32)
         for k in range(1, 4):
-            total = total + ref[k].astype(F32)
+            total = total + ref[c, k].astype(F32)
         return total
 
-    for mode in (0, 1):
-        across = y if mode == 0 else x
+    for mode, c in ((0, 0), (1, 0), (0, 1), (1, 1)):
+        if c == 0:
+            coefficients(mode)
+        analyse(mode, c)
+
+    for mode, c in ((0, 0), (1, 0), (0, 1), (1, 1)):
         for d in (1, 3, 2):
-            src = shift(across, d)
-            remote(
-                gs1[mode].at[src], gr1[mode].at[src], g1s.at[mode, d], g1r.at[mode, src], at(y, x, z, g)
-            ).wait_recv()
-        gs2[mode][...] = sum4(gr1[mode]).astype(BF16).reshape(4, 32, PIECE[mode] * 128)
-        gr2[mode][z] = gs2[mode][z]
+            first_sum(mode, c, d, True).wait_recv()
+        gs2[mode][c] = sum4(gr1[mode], c).astype(BF16).reshape(4, 16, PIECE[mode] * 128)
+        for d in (2, 1, 3):
+            begin(second_sum(mode, c, d, False))
+        gr2[mode][c, z] = gs2[mode][c, z]
+    tot[...] = jnp.zeros_like(tot)
+    for mode, c in ((0, 0), (1, 0), (0, 1), (1, 1)):
         for d in (1, 3, 2):
-            dest = shift(z, d)
-            send(
-                gs2[mode].at[dest], gr2[mode].at[z], g2s.at[mode, d], g2r.at[mode, z], at(y, x, dest, g)
-            )
-    for mode in (1, 0):
-        for d in (1, 3, 2):
-            src = shift(z, d)
-            remote(
-                gs2[mode].at[src], gr2[mode].at[src], g2s.at[mode, d], g2r.at[mode, src], at(y, x, z, g)
-            ).wait_recv()
-        tot[mode, :, 0 : PIECE[mode] * 128] = sum4(gr2[mode])
+            second_sum(mode, c, d, True).wait_recv()
+        tot[mode, c * 16 : c * 16 + 16, 0 : PIECE[mode] * 128] = sum4(gr2[mode], c)
 
     own_order = own_limit - 128.0 + lax.broadcasted_iota(jnp.int32, (16, 128), 1).astype(F32)
-    lane10 = lax.broadcasted_iota(jnp.int32, (10, 128), 1).astype(F32)
+    lane16 = lax.broadcasted_iota(jnp.int32, (16, 128), 1).astype(F32)
     for t in range(XT + YT):
         m, r0, c0 = where_packed(t)
-        value = tot[m, r0 : r0 + 10, c0 : c0 + 128]
+        value = jnp.concatenate(
+            [tot[m, c * 16 + r0 : c * 16 + r0 + 8, c0 : c0 + 128] for c in range(2)], axis=0
+        )
         if t > 0:
             cols = slice((t - 1) * 128, t * 128)
-            even = jnp.where(own_limit[0:10] <= 128.0 * t, value, 0.0)
+            even = jnp.where(own_limit <= 128.0 * t, value, 0.0)
             for k in range(OWN):
-                out[2 * k, :, cols] = even[2 * k : 2 * k + 2]
+                for c in range(2):
+                    out[2 * k, c : c + 1, cols] = even[8 * c + k : 8 * c + k + 1]
         if t < XT + YT - 1:
             s = 19 - t
             cols = slice(s * 128, s * 128 + 128)
             hi = value.astype(BF16)
             lo = (value - hi.astype(F32)).astype(BF16)
             back = nn(hi, flip[128:256, 0:128]) + nn(lo, flip[128:256, 0:128])
-            odd = jnp.where(own_order[0:10] + lane10 >= 2559.0 - 128.0 * s, back, 0.0)
+            odd = jnp.where(own_order + lane16 >= 2559.0 - 128.0 * s, back, 0.0)
             for k in range(OWN):
-                out[2 * k + 1, :, cols] = odd[2 * k : 2 * k + 2]
+                for c in range(2):
+                    out[2 * k + 1, c : c + 1, cols] = odd[8 * c + k : 8 * c + k + 1]
 
     for c in pending:
         c.wait_send()
@@ -744,8 +770,8 @@
         scratch_shapes=[pltpu.VMEM(o.shape, o.dtype) for o in operands]
         + [
             dma((len(operands),)),
-            pltpu.VMEM((2, 640, 2560), BF16),
-            pltpu.VMEM((2, 20, 16, 40, 128), F32),
+            pltpu.VMEM((2, 4, 4, 48, 2560), BF16),
+            pltpu.VMEM((2, 20, 16, 56, 128), F32),
             pltpu.VMEM((4, 2, 80, LANES[0]), BF16),
             pltpu.VMEM((4, 2, 80, LANES[1]), BF16),
             pltpu.VMEM((4, 2, 80, LANES[0]), BF16),
@@ -764,17 +790,17 @@
             pltpu.VMEM((2, 4, 4, 8, 128), F32),
             pltpu.VMEM((2, 1, 1, 256), F32),
             pltpu.VMEM((2, 4, 4, 1, 256), F32),
-            pltpu.VMEM((4, 80, 1024), F32),
+            pltpu.VMEM((2, 4, 80, 1024), F32),
             pltpu.VMEM((480, 512), BF16),
             pltpu.VMEM((480, 384), BF16),
-            pltpu.VMEM((4, 128, 512), BF16),
-            pltpu.VMEM((4, 128, 384), BF16),
-            pltpu.VMEM((4, 128, 512), BF16),
-            pltpu.VMEM((4, 128, 384), BF16),
-            pltpu.VMEM((4, 32, 512), BF16),
-            pltpu.VMEM((4, 32, 384), BF16),
-            pltpu.VMEM((4, 32, 512), BF16),
-            pltpu.VMEM((4, 32, 384), BF16),
+            pltpu.VMEM((2, 4, 64, 512), BF16),
+            pltpu.VMEM((2, 4, 64, 384), BF16),
+            pltpu.VMEM((2, 4, 64, 512), BF16),
+            pltpu.VMEM((2, 4, 64, 384), BF16),
+            pltpu.VMEM((2, 4, 16, 512), BF16),
+            pltpu.VMEM((2, 4, 16, 384), BF16),
+            pltpu.VMEM((2, 4, 16, 512), BF16),
+            pltpu.VMEM((2, 4, 16, 384), BF16),
             pltpu.VMEM((16, 1, 2048), F32),
             pltpu.VMEM((16, 640), F32),
             pltpu.VMEM((2, 4, 80, 128), F32),
@@ -785,9 +811,9 @@
             pltpu.VMEM((2, 32, 512), F32),
             pltpu.VMEM((32, 512), BF16),
             pltpu.VMEM((32, 384), BF16),
-            pltpu.VMEM((2, 32, 512), F32),
+            pltpu.VMEM((2, 40, 512), F32),
             pltpu.VMEM((160, 128), F32),
-            dma((2, 4)),
+            dma((4, 2, 4)),
             dma((2, 4, 2)),
             dma((2, 4, 2)),
             dma((2, 4)),
@@ -800,10 +826,10 @@
             dma((2, 4, 4)),
             dma((2, 4, 4)),
             dma((2, 4, 4)),
-            dma((2, 4)),
-            dma((2, 4)),
-            dma((2, 4)),
-            dma((2, 4)),
+            dma((2, 2, 4)),
+            dma((2, 2, 4)),
+            dma((2, 2, 4)),
+            dma((2, 2, 4)),
         ],
         compiler_params=pltpu.CompilerParams(
             collective_id=0, has_side_effects=True, vmem_limit_bytes=58 * 1024 * 1024

time: 79.4 us -> 73.4 us (0.924)
  Pallas kernels: 77.1 us -> 71.1 us
    pallas_call x1, Pallas kernels: 77.1 us -> 71.1 us  [per_device(): pl.pallas_call(kernel, out_shape=jax.ShapeDtypeStruct(white_noise.shape,...]
where the time goes in v3:
time: 73.4 us; the launch traced here: 72.8 us
  Pallas kernels  71.1 us (97%)
  other arithmetic  1.69 us (2%)
    pallas_call x1, Pallas kernels, per_device(): pl.pallas_call(kernel, out_shape=jax.ShapeDtypeStruct(white_noise.shape,...  71.1 us
    mul x1, other arithmetic, per_device(): return got * amplitude  1.69 us

profile of v3, /device:TPU:2, one launch (start us, length us, event | category | flops | bytes accessed | tf_op | source)
XLA Modules:
  0.0 72.8 jit_solution(9737159840460521106)
XLA Ops:
  0.0 0.0 copy-start
  0.0 71.1 %survey.1 = f32[10,2,2560]{2,1,0:T(2,128)} custom-call(bf16[2,640,2560]{2,1,0:T(8,128)(2,1)} %leg.1, s32[2560]{0:T(1024)} %refs_0_.1, bf16[640,2048]{1,0:T(8,128)(2,1)} %constant.34.clone.refs_1_, bf16[128,128]{1,0:T(8,128)(2,1)} %constant.35.clone.refs_2_, bf16[16,1024]{1,0:T(8,128)(2,1)} %constant.36.clone.refs_3_, f32[10,2,2560]{2,1,0:T(2,128)} %refs_4_.1, ...), custom_call_target="tpu_custom_call" | custom-call | tf_op jit(solution)/shard_map/survey/pallas_call | solution.py:765
  71.1 0.0 copy-done
  71.1 1.7 %broadcast_multiply_fusion = f32[10,2,2560]{2,1,0:T(2,128)} fusion(f32[10,2,2560]{2,1,0:T(2,128)} %survey.1, f32[2560]{0:T(1024)S(1)} %copy-done), kind=kLoop, calls=%fused_computation | loop fusion | flops 51200 | bytes 419840 | tf_op jit(solution)/shard_map/mul | solution.py:839
Async XLA Ops:
  0.0 71.1 %copy-start = (f32[2560]{0:T(1024)S(1)}, f32[2560]{0:T(1024)}, u32[]{:S(2)}) copy-start(f32[2560]{0:T(1024)} %refs_5_.1) | copy-start | bytes 30724

commit v4 on v3

--- a/solution.py
+++ b/solution.py
@@ -513,7 +513,7 @@
                 else:
                     frecv[mode, own, g] = fsend[mode, src, r]
             behind.append((mode, d))
-            if len(behind) > 4:
+            if len(behind) > 6:
                 scatter(*behind.pop(0))
     for mode, d in behind:
         scatter(mode, d)

time: 73.4 us -> 73.1 us (level)
  no operation moved by 1% of the time
where the time goes in v4:
time: 73.1 us; the launch traced here: 72.7 us
  Pallas kernels  71 us (97%)
  other arithmetic  1.69 us (2%)
    pallas_call x1, Pallas kernels, per_device(): pl.pallas_call(kernel, out_shape=jax.ShapeDtypeStruct(white_noise.shape,...  71 us
    mul x1, other arithmetic, per_device(): return got * amplitude  1.69 us

profile of v4, /device:TPU:2, one launch (start us, length us, event | category | flops | bytes accessed | tf_op | source)
XLA Modules:
  0.0 72.7 jit_solution(1752662779855014235)
XLA Ops:
  0.0 0.0 copy-start
  0.0 71.0 %survey.1 = f32[10,2,2560]{2,1,0:T(2,128)} custom-call(bf16[2,640,2560]{2,1,0:T(8,128)(2,1)} %leg.1, s32[2560]{0:T(1024)} %refs_0_.1, bf16[640,2048]{1,0:T(8,128)(2,1)} %constant.34.clone.refs_1_, bf16[128,128]{1,0:T(8,128)(2,1)} %constant.35.clone.refs_2_, bf16[16,1024]{1,0:T(8,128)(2,1)} %constant.36.clone.refs_3_, f32[10,2,2560]{2,1,0:T(2,128)} %refs_4_.1, ...), custom_call_target="tpu_custom_call" | custom-call | tf_op jit(solution)/shard_map/survey/pallas_call | solution.py:765
  71.0 0.0 copy-done
  71.0 1.7 %broadcast_multiply_fusion = f32[10,2,2560]{2,1,0:T(2,128)} fusion(f32[10,2,2560]{2,1,0:T(2,128)} %survey.1, f32[2560]{0:T(1024)S(1)} %copy-done), kind=kLoop, calls=%fused_computation | loop fusion | flops 51200 | bytes 419840 | tf_op jit(solution)/shard_map/mul | solution.py:839
Async XLA Ops:
  0.0 71.0 %copy-start = (f32[2560]{0:T(1024)S(1)}, f32[2560]{0:T(1024)}, u32[]{:S(2)}) copy-start(f32[2560]{0:T(1024)} %refs_5_.1) | copy-start | bytes 30724
